TPU v7x, 128 devices: a whole 4x4x4 slice. The times are simulated.
128 devices in a mesh: dom: 16 (over z, x), orient: 8 (over y, core).
Axes of the slice: x: 4, y: 4, z: 4, core: 2. Of those that a mesh axis runs over, the one named last changes fastest.
Arguments:
- images: bfloat16 [3072, 256, 256], P('dom'), may hold values from -400 to 400
- defocus: float32 [3072], P('dom'), may hold values from 2 to 12
- noise_var: float32 [256, 128], replicated, may hold values from 1 to 4
- references: bfloat16 [4, 64, 256, 256], P(None, 'orient', 'dom'), may hold values from -0.12 to 0.12
- orient_list: int32 [3072, 16], P('dom'), may hold values from 0 to 63, all different within a row
- class_label: int32 [3072], P('dom'), may hold values from 0 to 3
- owner: int32 [64, 256, 1], replicated, may hold values from 0 to 15; in each aligned block of 128 rows (0 to 127, 128 to 255, ..., all dimensions but the last counted through in order) at most 16 rows name the same one
- slab_row: int32 [64, 256], replicated, may hold values from 0 to 511
- kernel_index: int32 [64, 256], replicated, may hold values from 0 to 3
- interp: bfloat16 [4, 128, 128], replicated, may hold values from -0.5 to 0.5
Outputs:
- volume: float32 [8192, 4, 256], P(('dom', 'orient'))
- log_evidence: float32 [3072], P('dom')
Inputs may be any that keep to these rules, and one draw needn't show every extreme that they name: `orient_list`: each particle lists 16 distinct orientations. Taking slice rows in order of orientation then line, in each aligned block of 128 rows at most 16 rows name the same owner, and in every draw some owner is named by exactly 16 rows of some block.
All inputs are finite; a program needn't handle non-finite values.
Results may differ from a plain program's by a relative error of at most 0.022.
Values may be sent and summed in bfloat16 or wider, within the bound.
A program may use at most 256 MiB of HBM per device.

v0:
```python
import math

import jax
import jax.numpy as jnp
from jax import lax
from jax.sharding import PartitionSpec as P

SLAB_ROWS = 512


prior_hit = math.log(0.55)
prior_miss = math.log(0.15)
excluded = -1e30
block_lines = 32


def radius_sq(line_count, line_total, columns):
    row_pos = jnp.arange(line_count).astype(jnp.float32) - line_total // 2
    col_pos = jnp.arange(columns).astype(jnp.float32)
    halfway = float(line_total // 2)
    return (row_pos[:, None] * row_pos[:, None] + col_pos[None, :] * col_pos[None, :]) / (
        halfway * halfway
    )


def shift_waves(first_line, line_count, line_total, columns):
    row_pos = (first_line + jnp.arange(line_count)).astype(jnp.float32) - line_total // 2
    col_pos = jnp.arange(columns).astype(jnp.float32)
    offsets = jnp.arange(9)
    across = (offsets // 3 - 1).astype(jnp.float32)
    upward = (offsets % 3 - 1).astype(jnp.float32)
    phases = math.pi * (
        across[:, None, None] * col_pos[None, None, :] / columns
        + upward[:, None, None] * row_pos[None, :, None] / (line_total // 2)
    )
    return (jnp.cos(phases), jnp.sin(phases))


def choose_slots(owners_row, target, capacity):
    hits = owners_row == target
    ranking = jnp.cumsum(hits.astype(jnp.int32)) - 1
    return hits[None, :] & (ranking[None, :] == jnp.arange(capacity)[:, None])


def shards(
    images,
    defocus,
    noise_var,
    references,
    orient_list,
    class_label,
    owner,
    slab_row,
    kernel_index,
    interp,
):
    particles, line_total, row_width = images.shape
    columns = row_width // 2
    classes, group_size, line_share, ref_width = references.shape
    radius = radius_sq(line_total, line_total, columns)
    contrast = jnp.sin(defocus[:, None, None] * radius[None] + 0.3)
    factor = contrast / noise_var[None]
    weighted = (images * jnp.concatenate([factor, factor], axis=2)).astype(jnp.bfloat16)
    ctf_power = (contrast * factor).astype(jnp.bfloat16)
    segment = lax.all_gather(references, "dom", axis=2, tiled=True)
    span_lines = segment.shape[2]
    cosine, sine = shift_waves(jnp.int32(0), span_lines, line_total, columns)
    cosine_b = cosine[:, None, None]
    sine_b = sine[:, None, None]
    real_part = segment[..., :columns].astype(jnp.float32)
    imag_part = segment[..., columns:].astype(jnp.float32)
    shifted = jnp.concatenate(
        [
            real_part[None] * cosine_b - imag_part[None] * sine_b,
            imag_part[None] * cosine_b + real_part[None] * sine_b,
        ],
        axis=-1,
    ).astype(jnp.bfloat16)
    ref_power = (real_part * real_part + imag_part * imag_part).astype(jnp.bfloat16)
    local_weighted = weighted
    cross_term = jnp.einsum(
        "nlj,tkolj->ntko", local_weighted, shifted, preferred_element_type=jnp.float32
    )
    energy = jnp.einsum("nlc,kolc->nko", ctf_power, ref_power, preferred_element_type=jnp.float32)
    group = lax.axis_index("orient")
    wanted = group * group_size + jnp.arange(group_size)
    allowed = jnp.any(orient_list[:, :, None] == wanted[None, None, :], axis=1)
    prior = jnp.where(class_label[:, None] == jnp.arange(classes)[None, :], prior_hit, prior_miss)
    score = cross_term - 0.5 * energy[:, None] + prior[:, None, :, None]
    usable = jnp.broadcast_to(allowed[:, None, None, :], score.shape)
    masked = jnp.where(usable, score, excluded)
    local_peak = jnp.max(masked, axis=(1, 2, 3))
    peak_score = lax.pmax(local_peak, "orient")
    local_mass = jnp.sum(
        jnp.where(usable, jnp.exp(masked - peak_score[:, None, None, None]), 0.0), axis=(1, 2, 3)
    )
    total_mass = lax.psum(local_mass, "orient")
    log_evidence = peak_score + jnp.log(total_mass)
    posterior = jnp.where(
        usable,
        jnp.exp(masked - peak_score[:, None, None, None]) / total_mass[:, None, None, None],
        0.0,
    ).astype(jnp.bfloat16)

    def back_block(block_index, partial_value):
        first_line = block_index * block_lines
        local_weighted = lax.dynamic_slice_in_dim(weighted, first_line, block_lines, 1)
        stacked = jnp.einsum(
            "ntko,nlj->tkolj", posterior, local_weighted, preferred_element_type=jnp.float32
        )
        cosine, sine = shift_waves(first_line, block_lines, line_total, columns)
        cosine_b = cosine[:, None, None]
        sine_b = sine[:, None, None]
        real_part = stacked[..., :columns]
        imag_part = stacked[..., columns:]
        new_real = jnp.sum(real_part * cosine_b + imag_part * sine_b, axis=0)
        new_imag = jnp.sum(imag_part * cosine_b - real_part * sine_b, axis=0)
        return lax.dynamic_update_slice_in_dim(
            partial_value, jnp.concatenate([new_real, new_imag], axis=-1), first_line, 2
        )

    partial_value = lax.fori_loop(
        0,
        line_total // block_lines,
        back_block,
        jnp.zeros((classes, group_size, line_total, row_width), jnp.float32),
    )
    rounded = lax.optimization_barrier(partial_value.astype(jnp.bfloat16)).astype(jnp.float32)
    flat = rounded.reshape(classes, group_size * line_total, row_width)
    dom_count = lax.axis_size("dom")
    dom_index = lax.axis_index("dom")
    block_rows = group_size * line_total // dom_count
    capacity = 2 * block_rows // dom_count
    first_row = group * group_size
    owner_blocks = lax.dynamic_slice_in_dim(owner[:, :, 0], first_row, group_size, 0).reshape(
        dom_count, block_rows
    )
    slab_blocks = lax.dynamic_slice_in_dim(slab_row, first_row, group_size, 0).reshape(
        dom_count, block_rows
    )
    kernel_blocks = lax.dynamic_slice_in_dim(kernel_index, first_row, group_size, 0).reshape(
        dom_count, block_rows
    )
    incoming = jax.vmap(lambda owners_row: choose_slots(owners_row, dom_index, capacity))(
        owner_blocks
    )
    summed = lax.psum(flat.astype(jnp.bfloat16), "dom")
    summed = summed.reshape(classes, dom_count, block_rows, row_width)
    received = jnp.einsum(
        "sjr,ksrc->sjkc", incoming.astype(jnp.bfloat16), summed, preferred_element_type=jnp.float32
    ).astype(jnp.bfloat16)
    target_row = jnp.sum(jnp.where(incoming, slab_blocks[:, None, :], 0), axis=2).reshape(-1)
    kernel_slot = jnp.sum(jnp.where(incoming, kernel_blocks[:, None, :], 0), axis=2).reshape(-1)
    live_slot = jnp.any(incoming, axis=2).reshape(-1)
    slot_total = dom_count * capacity
    slots = received.reshape(slot_total, classes, 2, columns)
    every_kernel = jnp.einsum("mkxc,wcd->mwkxd", slots, interp, preferred_element_type=jnp.float32)
    picked = (kernel_slot[:, None] == jnp.arange(interp.shape[0])[None, :]).astype(jnp.float32)
    inserted = jnp.sum(every_kernel * picked[:, :, None, None, None], axis=1).astype(jnp.bfloat16)
    inserted = inserted.reshape(slot_total, classes * row_width)
    placement_map = (
        (target_row[None, :] == jnp.arange(SLAB_ROWS)[:, None]) & live_slot[None, :]
    ).astype(jnp.bfloat16)
    slab = jnp.dot(placement_map, inserted, preferred_element_type=jnp.float32).reshape(
        SLAB_ROWS, classes, row_width
    )
    volume = lax.psum_scatter(
        slab.astype(jnp.bfloat16), "orient", scatter_dimension=0, tiled=True
    ).astype(jnp.float32)
    return (volume, log_evidence)


def solution(mesh):
    return jax.shard_map(
        shards,
        mesh=mesh,
        in_specs=(
            P("dom", None, None),
            P("dom"),
            P(),
            P(None, "orient", "dom", None),
            P("dom", None),
            P("dom"),
            P(),
            P(),
            P(),
            P(),
        ),
        out_specs=(P(("dom", "orient"), None, None), P("dom")),
        check_vma=False,
    )
```

profile of v0, /device:TPU:1, one launch (start us, length us, event | category | flops | bytes accessed | tf_op | source)
XLA Modules:
  0.0 572.7 jit_solution(6637900940002616665)
XLA Ops:
  9.9 8.9 %fusion.23 = (f32[9,256,128]{2,0,1:T(8,128)}, f32[9,256,128]{2,0,1:T(8,128)}) fusion(f32[9,256]{0,1:T(8,128)S(1)} %copy.57, f32[9,128]{1,0:T(8,128)S(1)} %multiply_multiply_fusion.3), kind=kLoop, calls=%fused_computation.46 | loop fusion | flops 589824 | bytes 2373120 | tf_op jit(solution)/shard_map/cos | solution.py:36
  18.8 87.1 %fusion.16 = f32[192,256,128]{2,0,1:T(8,128)} fusion(f32[256,128]{1,0:T(8,128)} %param.14, f32[256,128]{1,0:T(8,128)S(1)} %add_multiply_fusion.2, f32[192]{0:T(256)} %param.13), kind=kLoop, calls=%fused_computation.36 | loop fusion | flops 18874368 | bytes 25428736 | tf_op jit(solution)/shard_map/div | solution.py:62
  105.9 33.5 %fusion.14 = bf16[192,256,256]{2,0,1:T(8,128)(2,1)} fusion(f32[192,256,128]{2,0,1:T(8,128)} %fusion.16, bf16[192,256,256]{2,1,0:T(8,128)(2,1)} %param.12), kind=kLoop, calls=%fused_computation.32 | loop fusion | flops 50331648 | bytes 75497472 | tf_op jit(solution)/shard_map/convert_element_type | solution.py:63
  142.5 91.7 %fusion.49 = f32[192,4,8]{0,2,1:T(8,128)S(1)} fusion(bf16[4,8,256,128]{3,2,1,0:T(8,128)(2,1)S(1)} %add_convert_fusion.1, f32[256,128]{1,0:T(8,128)S(1)} %add_multiply_fusion.2, f32[192]{0:T(256)S(1)} %copy-done.3, f32[256,128]{1,0:T(8,128)S(1)} %copy-done.2), kind=kOutput, calls=%fused_computation.54 | convolution fusion | flops 434116608 | bytes 2384640 | tf_op jit(solution)/shard_map/nlc,kolc->nko/dot_general | solution.py:84
  236.7 25.0 %subtract_convert_fusion = (bf16[9,4,8,256,128]{4,0,3,2,1:T(8,128)(2,1)}, bf16[9,4,8,256,128]{4,0,3,2,1:T(8,128)(2,1)}) fusion(f32[9,256,128]{2,0,1:T(8,128)} %get-tuple-element.173, f32[4,8,256,128]{3,2,1,0:T(8,128)} %get-tuple-element.171, f32[9,256,128]{2,0,1:T(8,128)} %get-tuple-element.172, f32[4,8,256,128]{3,2,1,0:T(8,128)S(1)} %get-tuple-element.170), kind=kLoop, calls=%fused_computation.30 | loop fusion | flops 75497472 | bytes 48496640 | tf_op jit(solution)/shard_map/convert
  261.7 31.0 %fusion.77 = (f32[192]{0:T(256)S(1)}, f32[192,9,4,8]{0,1,3,2:T(8,128)S(1)}) fusion(f32[192,4]{0,1:T(4,128)S(1)} %fusion.67, f32[192,4,8]{0,2,1:T(8,128)S(1)} %fusion.49, bf16[9,4,8,256,128]{4,0,3,2,1:T(8,128)(2,1)} %get-tuple-element.169, bf16[9,4,8,256,128]{4,0,3,2,1:T(8,128)(2,1)} %get-tuple-element.168, bf16[192,256,256]{2,0,1:T(8,128)(2,1)} %fusion.14, ...), kind=kOutput, calls=%fused_computation.102 | convolution fusion | flops 7323475968 | bytes 63165696 | tf_op jit(solution)/shard_map/nlj,tkolj->ntko/dot_general | solution.py:81
  292.8 13.5 %pmax.7 = f32[192]{0:T(256)S(1)} all-reduce(f32[192]{0:T(256)S(1)} %get-tuple-element.174), channel_id=1, replica_groups=mesh['dom'=16,'orient'=8] {'orient'}, use_global_device_ids=true, to_apply=%region_5.6 | all-reduce | flops 192 | bytes 1536 | tf_op jit(solution)/shard_map/pmax | solution.py:93
  306.4 14.7 %psum.14 = f32[192]{0:T(256)S(1)} all-reduce(f32[192]{0:T(256)S(1)} %select_reduce_fusion), channel_id=1, replica_groups=mesh['dom'=16,'orient'=8] {'orient'}, use_global_device_ids=true, to_apply=%region_7.8 | all-reduce | flops 192 | bytes 1536 | tf_op jit(solution)/shard_map/psum | solution.py:97
  323.6 98.0 %while.16 = (s32[]{:T(128)}, bf16[4,8,256,256]{3,2,1,0:T(8,128)(2,1)}, bf16[192,256,256]{2,0,1:T(8,128)(2,1)}, bf16[192,9,4,8]{0,1,3,2:T(8,128)(2,1)S(1)}, s32[]{:T(128)}, /*index=5*/s32[]{:T(128)}, s32[]{:T(128)}, s32[]{:T(128)}) while((s32[]{:T(128)}, bf16[4,8,256,256]{3,2,1,0:T(8,128)(2,1)}, bf16[192,256,256]{2,0,1:T(8,128)(2,1)}, ...), condition=%wide.region_11.12_spmd, body=%wide.region_8.11_spmd.sunk | while | flops 916270272 | bytes 25355040 | solution.py:122
  329.0 5.6 add_reduce_fusion.2
  337.0 4.2 convolution_bitcast_fusion.2
  341.3 5.6 add_reduce_fusion.2
  349.3 4.2 convolution_bitcast_fusion.2
  353.6 5.6 add_reduce_fusion.2
  365.8 5.6 add_reduce_fusion.2
  378.0 5.6 add_reduce_fusion.2
  390.3 5.6 add_reduce_fusion.2
  398.3 4.2 convolution_bitcast_fusion.2
  402.5 5.6 add_reduce_fusion.2
  410.6 4.2 convolution_bitcast_fusion.2
  414.8 5.6 add_reduce_fusion.2
  421.6 4.6 copy.60
  429.4 100.2 %all-reduce.2.cloned.1.call-done = bf16[4,16,128,256]{3,2,0,1:T(8,128)(2,1)} async-done(((bf16[4,16,128,256]{3,2,0,1:T(8,128)(2,1)}), bf16[4,16,128,256]{3,2,0,1:T(8,128)(2,1)}) %all-reduce.2.cloned.1.call-update) | async-done | bytes 4194320 | tf_op jit(solution)/shard_map/psum | solution.py:147
  535.6 28.5 %reduce-scatter.2.cloned.1.call-done = bf16[64,4,256]{2,0,1:T(8,128)(2,1)} async-done(((bf16[512,4,256]{2,0,1:T(8,128)(2,1)}), bf16[64,4,256]{2,0,1:T(8,128)(2,1)}) %reduce-scatter.2.cloned.1.call-update) | async-done | bytes 131088 | tf_op jit(solution)/shard_map/reduce_scatter | solution.py:167
  (122 shorter events, 57.4 us)
Async XLA Ops:
  7.2 525.4 %copy-start = (bf16[4,128,128]{2,1,0:T(8,128)(2,1)S(1)}, bf16[4,128,128]{2,1,0:T(8,128)(2,1)}, u32[]{:S(2)}) copy-start(bf16[4,128,128]{2,1,0:T(8,128)(2,1)} %param.21) | copy-start | bytes 393220
  7.2 132.2 %all-gather.2.cloned.1.call-start = ((), (), s32[]{:S(2)}) async-start(), calls=%async_computation.1 | async-start | bytes 4456448 | tf_op jit(solution)/shard_map/all_gather | solution.py:65
  7.9 521.6 %all-reduce.2.cloned.1.call-start = ((), (), s32[]{:S(2)}) async-start(), calls=%async_computation.2 | async-start | bytes 8388608 | tf_op jit(solution)/shard_map/psum | solution.py:147
  105.9 36.5 %copy-start.2 = (f32[256,128]{1,0:T(8,128)S(1)}, f32[256,128]{1,0:T(8,128)}, u32[]{:S(2)}) copy-start(f32[256,128]{1,0:T(8,128)} %param.14) | copy-start | bytes 393220
  105.9 36.5 %copy-start.3 = (f32[192]{0:T(256)S(1)}, f32[192]{0:T(256)}, u32[]{:S(2)}) copy-start(f32[192]{0:T(256)} %param.13) | copy-start | bytes 2308
  142.5 91.7 %copy-start.1 = (bf16[4,8,256,256]{3,2,1,0:T(8,128)(2,1)S(1)}, bf16[4,8,256,256]{3,2,1,0:T(8,128)(2,1)}, u32[]{:S(2)}) copy-start(bf16[4,8,256,256]{3,2,1,0:T(8,128)(2,1)} %all-gather.2.cloned.1.call-done) | copy-start | bytes 12582916
  426.3 137.8 %reduce-scatter.2.cloned.1.call-start = ((), (), s32[]{:S(2)}) async-start(), calls=%async_computation.3 | async-start | bytes 1179648 | tf_op jit(solution)/shard_map/reduce_scatter | solution.py:167
Sparse Core Ops, SparseCore 0:
  10.1 60.0 all-gather.1
  426.4 103.0 all-reduce.1
  535.1 28.9 reduce-scatter.1
where the time goes:
time: 584 us; the launch traced here: 573 us
  other arithmetic  220 us (38%)
  matrix products  162 us (28%)
  waiting for transfers between devices  129 us (22%)
  blocking collectives  28.1 us (5%)
  local copies, waits for them, and re-layouts  19.3 us (3%)
  between operations  14.3 us (2%)
    psum x1, waiting for transfers between devices, shards(): summed = lax.psum(flat.astype(jnp.bfloat16), 'dom')  100 us
    dot_general x1, matrix products, shards(): jnp.einsum('nlc,kolc->nko', ctf_power, ref_power, preferred_element_type=...  91.7 us
    div x1, other arithmetic, shards(): factor = contrast / noise_var[None]  87.1 us
    reduce_sum x8, other arithmetic, back_block(): new_real = jnp.sum(real_part * cosine_b + imag_part * sine_b, axis=0)  45.2 us
    dot_general x8, matrix products, back_block(): jnp.einsum('ntko,nlj->tkolj', posterior, local_weighted, preferred_elemen...  33.8 us
    convert_element_type x1, other arithmetic, shards(): (images * jnp.concatenate([factor, factor], axis=2)).astype(jnp.bfloat16)  33.5 us
    dot_general x1, matrix products, shards(): jnp.einsum('nlj,tkolj->ntko', local_weighted, shifted, preferred_element_...  31 us
    reduce_scatter x1, waiting for transfers between devices, shards(): lax.psum_scatter(slab.astype(jnp.bfloat16), 'orient', scatter_dimension=0...  28.5 us
  transfers between devices with their start and end apart: 3, of which 2 were waited for; matrix products, arithmetic and copies ran while one was open for 24% of the time, Pallas kernels for 0%

commit v1 on v0

v1 whole, which is shorter than its diff:
```python
import functools
import math

import jax
import jax.numpy as jnp
import numpy as np
from jax import lax
from jax.experimental import pallas as pl
from jax.experimental.pallas import tpu as pltpu
from jax.sharding import PartitionSpec as P

SLAB_ROWS = 512
LINES = 256
COLS = 128
WIDE = 2 * COLS
N = 192
CL = 4
OG = 8
KO = CL * OG
PL = 16
NP = LINES // PL
PK = PL * WIDE
SIDE = 4
GROUPS = 8
BASES = 9
CAP = 16

prior_hit = math.log(0.55)
prior_miss = math.log(0.15)
excluded = -1e30
MESH = pl.DeviceIdType.MESH
bf16 = jnp.bfloat16
f32 = jnp.float32

ORDER = (
    (0, 0), (0, 1), (0, 3), (1, 0), (3, 0), (1, 1), (1, 3), (3, 1), (3, 3),
    (0, 2), (2, 0), (1, 2), (3, 2), (2, 1), (2, 3), (2, 2),
)


def gather_plan():
    msgs = []
    for first, lo in (("x", 0), ("z", PL // 2)):
        mid, hi = lo + PL // 4, lo + PL // 2
        second = "z" if first == "x" else "x"

        def rel(f, s):
            return (s, f) if first == "x" else (f, s)

        msgs += [(0, rel(0, 0), lo, hi, first, d) for d in (1, -1)]
        msgs += [(1, rel(1, 0), lo, mid, first, -1), (1, rel(3, 0), mid, hi, first, 1)]
        for rank, f in ((0.5, 0), (2, 1), (2, 3), (4, 2)):
            msgs += [(rank, rel(f, 0), lo, hi, second, d) for d in (1, -1)]
            msgs += [
                (rank + 1, rel(f, 1), lo, mid, second, -1),
                (rank + 1, rel(f, 3), mid, hi, second, 1),
            ]
    msgs.sort(key=lambda m: m[0])
    msgs = [m[1:] for m in msgs]

    def landing(m):
        (dz, dx), lo, hi, axis, d = m
        return ((dz, (dx - d) % 4) if axis == "x" else ((dz - d) % 4, dx), lo, hi)

    land = [landing(m) for m in msgs]
    early = {
        1: [(0, 1, 0), (0, 3, 0), (1, 0, 1), (3, 0, 1), (0, 1, 1), (0, 3, 1), (1, 0, 0), (3, 0, 0)],
        3: [(0, 2, 0), (2, 0, 1)],
        5: [(1, 1, 0), (3, 1, 0), (1, 3, 0), (3, 3, 0), (1, 1, 1), (1, 3, 1), (3, 1, 1), (3, 3, 1)],
        10: [(1, 2, 0), (3, 2, 0), (2, 1, 1), (2, 3, 1)],
    }
    have = {((0, 0), line) for line in range(PL)}
    waited, sent, steps = set(), set(), []

    def ready(m):
        return all((m[0], line) in have for line in range(m[1], m[2]))

    for step in range(NP):
        acts = []
        if step == 0:
            for i, m in enumerate(msgs):
                if ready(m):
                    acts.append(("send", i))
                    sent.add(i)
        wanted = [((dz, dx), half) for dz, dx, half in early.get(step, [])]
        wanted += [(ORDER[step], half) for half in (0, 1)] if step else []
        for piece, half in wanted:
            for i, (at, lo, hi) in enumerate(land):
                if at == piece and lo // (PL // 2) == half and i not in waited:
                    waited.add(i)
                    acts.append(("wait", i))
                    have |= {(at, line) for line in range(lo, hi)}
            for i, m in enumerate(msgs):
                if i not in sent and ready(m):
                    acts.append(("send", i))
                    sent.add(i)
        steps.append(acts)
    assert len(waited) == len(msgs) == len(sent)
    return msgs, land, steps


MSGS, LAND, STEPS = gather_plan()


def fine_sin(angle):
    turns = jnp.floor(angle * (1.0 / math.pi) + 0.5)
    x = angle - turns * 3.140625
    x = x - turns * (math.pi - 3.140625)
    odd = turns - 2.0 * jnp.floor(turns * 0.5)
    x2 = x * x
    poly = -1.0 / 39916800.0
    for c in (1.0 / 362880.0, -1.0 / 5040.0, 1.0 / 120.0, -1.0 / 6.0):
        poly = poly * x2 + c
    s = x + x * x2 * poly
    return s * (1.0 - 2.0 * odd)


def pick(step, values):
    out = jnp.int32(0)
    for i, v in enumerate(values):
        if v:
            out = out + jnp.where(step == i, v, 0)
    return out


def score_kernel(
    refs_ref, images_hbm, focus_ref, noise_ref, list_ref, label_ref, rowtab_ref, offs_ref, coltab_ref, lines_ref,
    post_ref, evid_ref, weighted_hbm,
    refs_all, ibuf, fre, fim, wbuf, cbuf, sbuf, rbuf, acc, eacc, colsin, colcos, angtab, sc, stats,
    send_sem, recv_sem, ssend_sem, srecv_sem, in_sem, out_sem,
):
    dom = lax.axis_index("dom")
    group = lax.axis_index("orient")
    z, x = dom // SIDE, dom % SIDE

    def origin(dz, dx):
        return ((z + dz) % SIDE) * SIDE + (x + dx) % SIDE

    def step_origin(step):
        return origin(pick(step, [o[0] for o in ORDER]), pick(step, [o[1] for o in ORDER]))

    def image_copy(step):
        lines = pl.ds(pl.multiple_of(step_origin(step) * PL, PL), PL)
        return pltpu.make_async_copy(images_hbm.at[:, lines, :], ibuf.at[step % 2], in_sem.at[step % 2])

    def weighted_copy(step):
        return pltpu.make_async_copy(wbuf.at[step % 2], weighted_hbm.at[step_origin(step)], out_sem.at[step % 2])

    image_copy(0).start()

    barrier = pltpu.get_barrier_semaphore()
    for dz, dx in ((0, 1), (0, 3), (1, 0), (3, 0)):
        pl.semaphore_signal(barrier, inc=1, device_id=(origin(dz, dx), group), device_id_type=MESH)
    for k in range(1, GROUPS):
        pl.semaphore_signal(barrier, inc=1, device_id=(dom, (group + k) % GROUPS), device_id_type=MESH)
    pl.semaphore_wait(barrier, 4 + GROUPS - 1)

    def message(i):
        (dz, dx), lo, hi, axis, d = MSGS[i]
        to = origin(0, d % 4) if axis == "x" else origin(d % 4, 0)
        at = origin(dz, dx)
        rows = refs_all.at[at, pl.ds(lo, hi - lo)]
        src = refs_ref.at[pl.ds(lo, hi - lo)] if (dz, dx) == (0, 0) else rows
        return pltpu.make_async_remote_copy(
            src_ref=src, dst_ref=rows, send_sem=send_sem.at[i], recv_sem=recv_sem.at[i],
            device_id=(to, group), device_id_type=MESH,
        )

    def arrival(i):
        (dz, dx), lo, hi = LAND[i]
        rows = refs_all.at[origin(dz, dx), pl.ds(lo, hi - lo)]
        axis, d = MSGS[i][3:]
        frm = origin(0, -d % 4) if axis == "x" else origin(-d % 4, 0)
        return pltpu.make_async_remote_copy(
            src_ref=rows, dst_ref=rows, send_sem=send_sem.at[i], recv_sem=recv_sem.at[i],
            device_id=(frm, group), device_id_type=MESH,
        )

    def traffic(acts):
        for kind, i in acts:
            if kind == "send":
                message(i).start()
            else:
                arrival(i).wait_recv()

    traffic(STEPS[0])
    refs_all[dom] = refs_ref[...]
    focus = focus_ref[...]
    colang = focus[:, 0:1] * coltab_ref[0:1, :]
    colsin[...] = fine_sin(colang)
    colcos[...] = fine_sin(colang + math.pi / 2)
    acc[...] = jnp.zeros_like(acc)
    eacc[...] = jnp.zeros_like(eacc)

    def one_share(step, carry):
        for i in range(1, NP):
            if STEPS[i]:
                pl.when(step == i)(functools.partial(traffic, STEPS[i]))
        share = step_origin(step)
        slot = step % 2
        pl.when(step + 1 < NP)(lambda: image_copy(step + 1).start())
        angtab[...] = fine_sin(focus_ref[...] * rowtab_ref[share, 0:1, :] + offs_ref[0:1, :])
        image_copy(step).wait()

        def widen(i, c):
            part = ibuf[slot, pl.ds(pl.multiple_of(i * 8, 8), 8)].astype(f32)
            part = part.reshape(128, WIDE)
            rows = pl.ds(pl.multiple_of(i * 128, 128), 128)
            fre[rows, :] = part[:, :COLS]
            fim[rows, :] = part[:, COLS:]
            return c

        lax.fori_loop(0, N // 8, widen, 0)
        pl.when(step >= 2)(lambda: weighted_copy(step - 2).wait())

        def weigh(i, c):
            rows = pl.ds(pl.multiple_of(i * 32, 32), 32)
            cs, cc = colsin[rows, :], colcos[rows, :]
            ang = angtab[rows, :]
            for j in range(PL):
                inv = 1.0 / noise_ref[share, j : j + 1, :]
                con = ang[:, j : j + 1] * cc + ang[:, PL + j : PL + j + 1] * cs
                fac = con * inv
                take = pl.ds(i * (32 * PL) + j, 32, stride=PL)
                wbuf[slot, rows, j * WIDE : j * WIDE + COLS] = (fre[take, :] * fac).astype(bf16)
                wbuf[slot, rows, j * WIDE + COLS : (j + 1) * WIDE] = (fim[take, :] * fac).astype(bf16)
                cbuf[rows, j * COLS : (j + 1) * COLS] = (con * fac).astype(bf16)
            return c

        lax.fori_loop(0, N // 32, weigh, 0)
        weighted_copy(step).start()

        ca, sa = coltab_ref[1:2, :], coltab_ref[2:3, :]
        for j in range(PL):
            ref = refs_all[share, j].astype(f32)
            re, im = ref[:, :COLS], ref[:, COLS:]
            cp, sp = lines_ref[share, j : j + 1, :], lines_ref[share, PL + j : PL + j + 1, :]
            rbuf[:, j * COLS : (j + 1) * COLS] = (re * re + im * im).astype(bf16)
            for a, (r, m) in enumerate(((re, im), (re * ca, im * ca), (im * -sa, re * sa))):
                for b, (r2, m2) in enumerate(((r, m), (r * cp, m * cp), (m * -sp, r * sp))):
                    at = (a * 3 + b) * KO
                    sbuf[at : at + KO, j * WIDE : j * WIDE + COLS] = r2.astype(bf16)
                    sbuf[at : at + KO, j * WIDE + COLS : (j + 1) * WIDE] = m2.astype(bf16)
        nt = (((1,), (1,)), ((), ()))
        acc[...] += lax.dot_general(sbuf[...], wbuf[slot], nt, preferred_element_type=f32)
        eacc[...] += lax.dot_general(rbuf[...], cbuf[...], nt, preferred_element_type=f32)
        return carry

    lax.fori_loop(0, NP, one_share, 0)

    def band(ref, i):
        return ref[i * KO : (i + 1) * KO, :]

    row = lax.broadcasted_iota(jnp.int32, (KO, N), 0)
    wanted = group * OG + row // CL
    hits = jnp.zeros((KO, N), f32)
    for j in range(list_ref.shape[0]):
        hits = jnp.where(list_ref[j : j + 1, :] == wanted, 1.0, hits)
    usable = hits > 0.5
    base = jnp.where(label_ref[0:1, :] == row % CL, prior_hit, prior_miss) - 0.5 * eacc[...]
    xs = [[band(acc, a * 3 + b) for b in range(3)] for a in range(3)]
    peak = jnp.full((KO, N), excluded, f32)
    for t in range(BASES):
        a, b = t // 3 - 1, t % 3 - 1

        def along(row_):
            return row_[0] if b == 0 else row_[1] + b * row_[2]

        cross = along(xs[0]) if a == 0 else along(xs[1]) + a * along(xs[2])
        score = jnp.where(usable, cross + base, excluded)
        sc[t * KO : (t + 1) * KO, :] = score
        peak = jnp.maximum(peak, score)
    peak = jnp.max(peak, axis=0, keepdims=True)
    mass = jnp.zeros((KO, N), f32)
    for t in range(BASES):
        mass = mass + jnp.where(usable, jnp.exp(band(sc, t) - peak), 0.0)
    mass = jnp.sum(mass, axis=0, keepdims=True)
    stats[group, 0:8, :] = jnp.broadcast_to(peak, (8, N))
    stats[group, 8:16, :] = jnp.broadcast_to(mass, (8, N))

    def stat_copy(k, slot_group, to):
        mine = stats.at[slot_group]
        return pltpu.make_async_remote_copy(
            src_ref=mine, dst_ref=mine, send_sem=ssend_sem.at[k], recv_sem=srecv_sem.at[k],
            device_id=(dom, to), device_id_type=MESH,
        )

    for k in range(1, GROUPS):
        stat_copy(k, group, (group + k) % GROUPS).start()
    for k in range(1, GROUPS):
        frm = (group + GROUPS - k) % GROUPS
        stat_copy(k, frm, frm).wait_recv()
    top = stats[0, 0:1, :]
    for g in range(1, GROUPS):
        top = jnp.maximum(top, stats[g, 0:1, :])
    total = jnp.zeros((1, N), f32)
    for g in range(GROUPS):
        total = total + stats[g, 8:9, :] * jnp.exp(stats[g, 0:1, :] - top)
    evid_ref[...] = top + jnp.log(total)
    scale = 1.0 / total
    ps = [
        [jnp.where(usable, jnp.exp(band(sc, a * 3 + b) - top) * scale, 0.0) for b in range(3)]
        for a in range(3)
    ]
    basis = []
    for less, none, more in ps:
        basis.append((none, more + less, more - less))
    for b in range(3):
        less, none, more = basis[0][b], basis[1][b], basis[2][b]
        for a, v in enumerate((none, more + less, more - less)):
            post_ref[(a * 3 + b) * KO : (a * 3 + b + 1) * KO, :] = v.astype(bf16)

    weighted_copy(NP - 2).wait()
    weighted_copy(NP - 1).wait()
    for i in range(len(MSGS)):
        message(i).wait_send()
    for k in range(1, GROUPS):
        stat_copy(k, group, (group + k) % GROUPS).wait_send()


CHUNKS = 4
ROWS = 32 * CL
HALF = ROWS // 2
QUART = ROWS // 4


def back_kernel(
    post_ref, weighted_hbm, coltab_ref, lines_ref,
    out_ref,
    wbuf, part, r1, r2, p2, q1, q2,
    in_sem, send_sem, recv_sem,
):
    dom = lax.axis_index("dom")
    group = lax.axis_index("orient")
    z, x = dom // SIDE, dom % SIDE

    def neighbour(axis, d):
        return z * SIDE + (x + d) % SIDE if axis == "x" else ((z + d) % SIDE) * SIDE + x

    def share_of(i):
        return 2 * (i // 4) + i % 2 + 8 * ((i % 4) // 2)

    def load(i):
        return pltpu.make_async_copy(weighted_hbm.at[share_of(i)], wbuf.at[i % 3], in_sem.at[i % 3])

    load(0).start()
    load(1).start()
    barrier = pltpu.get_barrier_semaphore()
    for axis in ("x", "z"):
        for d in (1, 3):
            pl.semaphore_signal(barrier, inc=1, device_id=(neighbour(axis, d), group), device_id_type=MESH)
    pl.semaphore_wait(barrier, 4)

    ca, sa = coltab_ref[1:2, :], coltab_ref[2:3, :]

    def compute(i):
        load(i).wait()
        pl.when(i + 2 < NP)(lambda: load(i + 2).start())
        chunk, half, share = i // 4, (i % 4) // 2, share_of(i)
        for four in range(PL // 4):
            outs = []
            for j in range(four * 4, four * 4 + 4):
                g = jnp.dot(
                    post_ref[...], wbuf[i % 3, :, j * WIDE : (j + 1) * WIDE], preferred_element_type=f32
                )
                cp, sp = lines_ref[share, j : j + 1, :], lines_ref[share, PL + j : PL + j + 1, :]
                vs = []
                for a in range(3):
                    g0, gc, gs = (g[(a * 3 + b) * KO : (a * 3 + b + 1) * KO, :] for b in range(3))
                    vs.append(
                        (
                            g0[:, :COLS] + gc[:, :COLS] * cp + gs[:, COLS:] * sp,
                            g0[:, COLS:] + gc[:, COLS:] * cp - gs[:, :COLS] * sp,
                        )
                    )
                outs.append(
                    jnp.concatenate(
                        [
                            vs[0][0] + vs[1][0] * ca + vs[2][1] * sa,
                            vs[0][1] + vs[1][1] * ca - vs[2][0] * sa,
                        ],
                        axis=1,
                    )
                )
            row = pl.multiple_of((i % 2) * (PL * CL) + four * 16, 16)
            for o in range(OG):
                piece = jnp.concatenate([v[o * CL : (o + 1) * CL, :] for v in outs], axis=0)
                part[chunk, o // 2, (o % 2) * 2 + half, pl.ds(row, 16), :] = piece.astype(bf16)

    def setup(h):
        first, second = ("x", "z") if h == 0 else ("z", "x")
        return (first, x, second, z) if h == 0 else (first, z, second, x)

    def column(c, h, f, lo, size):
        rows = pl.ds(h * HALF + lo, size)
        return part.at[c, :, f, rows, :] if h == 0 else part.at[c, f, :, rows, :]

    def copy(src, dst, c, idx, axis, d):
        return pltpu.make_async_remote_copy(
            src_ref=src, dst_ref=dst, send_sem=send_sem.at[c, idx], recv_sem=recv_sem.at[c, idx],
            device_id=(neighbour(axis, d), group), device_id_type=MESH,
        )

    def copies(c, h, stage):
        first, f, second, s = setup(h)
        far_f, far_s = (f + 2) % 4, (s + 2) % 4
        out = []
        for n_, d in enumerate((3, 1)):
            idx = (h * 4 + stage) * 2 + n_
            if stage == 0:
                out.append(copy(column(c, h, far_f, n_ * QUART, QUART), r1.at[c, h, n_], c, idx, first, d))
            elif stage == 1:
                out.append(copy(column(c, h, (f + d) % 4, 0, HALF), r2.at[c, h, n_], c, idx, first, d))
            elif stage == 2:
                src = p2.at[c, h, far_s, pl.ds(n_ * QUART, QUART), :]
                out.append(copy(src, q1.at[c, h, n_], c, idx, second, d))
            else:
                out.append(copy(p2.at[c, h, (s + d) % 4], q2.at[c, h, n_], c, idx, second, d))
        return out

    def column_get(c, h, f, i, lo, size):
        rows = pl.ds(h * HALF + lo, size)
        return part[c, i, f, rows, :] if h == 0 else part[c, f, i, rows, :]

    def column_set(c, h, f, i, lo, size, value):
        rows = pl.ds(h * HALF + lo, size)
        if h == 0:
            part[c, i, f, rows, :] = value
        else:
            part[c, f, i, rows, :] = value

    def advance(c, stage):
        for h in (0, 1):
            first, f, second, s = setup(h)
            if stage > 0:
                for cp_ in copies(c, h, stage - 1):
                    cp_.wait_recv()
            if stage == 1:
                for n_, d in enumerate((3, 1)):
                    for i in range(SIDE):
                        to = (f + d) % 4
                        mine = column_get(c, h, to, i, n_ * QUART, QUART).astype(f32)
                        new = mine + r1[c, h, n_, i].astype(f32)
                        column_set(c, h, to, i, n_ * QUART, QUART, new.astype(bf16))
            elif stage == 2:
                for i in range(SIDE):
                    new = column_get(c, h, f, i, 0, HALF).astype(f32)
                    new = new + r2[c, h, 0, i].astype(f32) + r2[c, h, 1, i].astype(f32)
                    p2[c, h, i] = new.astype(bf16)
            elif stage == 3:
                for n_, d in enumerate((3, 1)):
                    rows = pl.ds(n_ * QUART, QUART)
                    to = (s + d) % 4
                    new = p2[c, h, to, rows, :].astype(f32) + q1[c, h, n_].astype(f32)
                    p2[c, h, to, rows, :] = new.astype(bf16)
            elif stage == 4:
                new = p2[c, h, s].astype(f32) + q2[c, h, 0].astype(f32) + q2[c, h, 1].astype(f32)
                out_ref[pl.ds(pl.multiple_of(c * ROWS, ROWS) + h * HALF, HALF), :] = new.astype(bf16)
            if stage < 4:
                for cp_ in copies(c, h, stage):
                    cp_.start()

    def tick(t, carry):
        @pl.when(t < CHUNKS)
        def _():
            def body(q, c):
                compute(t * 4 + q)
                return c

            lax.fori_loop(0, 4, body, 0)

        for stage in range(5):
            c = t - stage
            pl.when((c >= 0) & (c < CHUNKS))(functools.partial(advance, c, stage))
        return carry

    lax.fori_loop(0, CHUNKS + 4, tick, 0)
    for c in range(CHUNKS):
        for h in (0, 1):
            for stage in range(4):
                for cp_ in copies(c, h, stage):
                    cp_.wait_send()


VM = pl.BlockSpec(memory_space=pltpu.VMEM)
ANY = pl.BlockSpec(memory_space=pl.ANY)


def constants():
    c = np.arange(COLS, dtype=np.float32)
    l = np.arange(LINES, dtype=np.float32) - LINES // 2
    half = float(LINES // 2)
    coltab = np.zeros((8, COLS), np.float32)
    coltab[0] = c * c / (half * half)
    coltab[1] = np.cos(math.pi * c / COLS)
    coltab[2] = np.sin(math.pi * c / COLS)
    rowtab = np.zeros((NP, 8, COLS), np.float32)
    rsq = (l * l / (half * half)).reshape(NP, 1, PL)
    rowtab[:, :, :PL] = rsq
    rowtab[:, :, PL : 2 * PL] = rsq
    offs = np.zeros((8, COLS), np.float32)
    offs[:, :PL] = 0.3
    offs[:, PL : 2 * PL] = 0.3 + math.pi / 2
    ang = (math.pi * l / half).reshape(NP, PL, 1)
    lines = np.concatenate([np.cos(ang), np.sin(ang)], axis=1)
    lines = np.broadcast_to(lines, (NP, 2 * PL, COLS)).astype(np.float32)
    return coltab, rowtab, offs, lines


def shards(
    images, defocus, noise_var, references, orient_list, class_label, owner, slab_row, kernel_index, interp
):
    coltab, rowtab, offs, lines = (jnp.asarray(a) for a in constants())
    refs = jnp.transpose(references, (2, 1, 0, 3)).reshape(PL, KO, WIDE)
    focus = jnp.broadcast_to(defocus[:, None], (N, COLS))
    labels = jnp.broadcast_to(class_label[None, :], (8, N))
    post, evidence, weighted = pl.pallas_call(
        score_kernel,
        out_shape=(
            jax.ShapeDtypeStruct((BASES * KO, N), bf16),
            jax.ShapeDtypeStruct((1, N), f32),
            jax.ShapeDtypeStruct((NP, N, PK), bf16),
        ),
        in_specs=[VM, ANY] + [VM] * 8,
        out_specs=(VM, VM, ANY),
        scratch_shapes=[
            pltpu.VMEM((NP, PL, KO, WIDE), bf16),
            pltpu.VMEM((2, N, PL, WIDE), bf16),
            pltpu.VMEM((N * PL, COLS), f32),
            pltpu.VMEM((N * PL, COLS), f32),
            pltpu.VMEM((2, N, PK), bf16),
            pltpu.VMEM((N, PL * COLS), bf16),
            pltpu.VMEM((BASES * KO, PK), bf16),
            pltpu.VMEM((KO, PL * COLS), bf16),
            pltpu.VMEM((BASES * KO, N), f32),
            pltpu.VMEM((KO, N), f32),
            pltpu.VMEM((N, COLS), f32),
            pltpu.VMEM((N, COLS), f32),
            pltpu.VMEM((N, COLS), f32),
            pltpu.VMEM((BASES * KO, N), f32),
            pltpu.VMEM((GROUPS, 16, N), f32),
            pltpu.SemaphoreType.DMA((len(MSGS),)),
            pltpu.SemaphoreType.DMA((len(MSGS),)),
            pltpu.SemaphoreType.DMA((GROUPS,)),
            pltpu.SemaphoreType.DMA((GROUPS,)),
            pltpu.SemaphoreType.DMA((2,)),
            pltpu.SemaphoreType.DMA((2,)),
        ],
        compiler_params=pltpu.CompilerParams(
            collective_id=0, has_side_effects=True, vmem_limit_bytes=40 * 2**20
        ),
    )(
        refs, images, focus, noise_var.reshape(NP, PL, COLS), orient_list.T, labels, rowtab, offs, coltab, lines
    )
    block = pl.pallas_call(
        back_kernel,
        out_shape=jax.ShapeDtypeStruct((CHUNKS * ROWS, WIDE), bf16),
        in_specs=[VM, ANY, VM, VM],
        out_specs=VM,
        scratch_shapes=[
            pltpu.VMEM((3, N, PK), bf16),
            pltpu.VMEM((CHUNKS, SIDE, SIDE, ROWS, WIDE), bf16),
            pltpu.VMEM((CHUNKS, 2, 2, SIDE, QUART, WIDE), bf16),
            pltpu.VMEM((CHUNKS, 2, 2, SIDE, HALF, WIDE), bf16),
            pltpu.VMEM((CHUNKS, 2, SIDE, HALF, WIDE), bf16),
            pltpu.VMEM((CHUNKS, 2, 2, QUART, WIDE), bf16),
            pltpu.VMEM((CHUNKS, 2, 2, HALF, WIDE), bf16),
            pltpu.SemaphoreType.DMA((3,)),
            pltpu.SemaphoreType.DMA((CHUNKS, 16)),
            pltpu.SemaphoreType.DMA((CHUNKS, 16)),
        ],
        compiler_params=pltpu.CompilerParams(
            collective_id=1, has_side_effects=True, vmem_limit_bytes=40 * 2**20
        ),
    )(post, weighted, coltab, lines)

    group = lax.axis_index("orient")
    dom = lax.axis_index("dom")
    half_lines = LINES // 2

    def group_rows(a):
        return lax.dynamic_slice_in_dim(a, group * OG, OG, 0).reshape(NP, half_lines)

    owners, slabs, kernels = group_rows(owner[:, :, 0]), group_rows(slab_row), group_rows(kernel_index)
    mine = lax.dynamic_slice_in_dim(kernels, dom, 1, 0)[0]
    rows = block.reshape(half_lines, CL * 2, COLS)
    every = jnp.einsum("rxc,wcd->rwxd", rows, interp, preferred_element_type=f32)
    inserted = jnp.zeros(rows.shape, f32)
    for w in range(interp.shape[0]):
        inserted = jnp.where((mine == w)[:, None, None], every[:, w], inserted)
    inserted = inserted.astype(bf16).reshape(half_lines, CL * WIDE)
    earlier = np.tril(np.ones((half_lines, half_lines), bool), -1)
    rank = jnp.sum((owners[:, :, None] == owners[:, None, :]) & earlier[None], axis=2).astype(jnp.int32)
    own_mine = lax.dynamic_slice_in_dim(owners, dom, 1, 0)[0]
    rank_mine = lax.dynamic_slice_in_dim(rank, dom, 1, 0)[0]
    slot_ids = jnp.arange(NP * CAP)
    sendmap = ((own_mine * CAP + rank_mine)[None, :] == slot_ids[:, None]).astype(bf16)
    outgoing = jnp.dot(sendmap, inserted, preferred_element_type=f32).astype(bf16)
    received = lax.all_to_all(outgoing, "dom", 0, 0, tiled=True)
    live = (owners[:, None, :] == dom) & (rank[:, None, :] == jnp.arange(CAP)[None, :, None])
    target = jnp.max(jnp.where(live, slabs[:, None, :], -1), axis=2).reshape(-1)
    placement = (target[None, :] == jnp.arange(SLAB_ROWS)[:, None]).astype(bf16)
    slab = jnp.dot(placement, received, preferred_element_type=f32)
    slab = slab.reshape(SLAB_ROWS, CL, WIDE).astype(bf16)
    volume = lax.psum_scatter(slab, "orient", scatter_dimension=0, tiled=True).astype(f32)
    return volume, evidence.reshape(N)


def solution(mesh):
    return jax.shard_map(
        shards,
        mesh=mesh,
        in_specs=(
            P("dom", None, None),
            P("dom"),
            P(),
            P(None, "orient", "dom", None),
            P("dom", None),
            P("dom"),
            P(),
            P(),
            P(),
            P(),
        ),
        out_specs=(P(("dom", "orient"), None, None), P("dom")),
        check_vma=False,
    )
```

time: 584 us -> 180 us (0.31); the launches traced: 573 us -> 177 us
  other arithmetic: 220 us -> 1.24 us
  matrix products: 162 us -> 3.03 us
  Pallas kernels: 0 us -> 103 us
  waiting for transfers between devices: 129 us -> 38.7 us
  blocking collectives: 28.1 us -> 0 us
  local copies, waits for them, and re-layouts: 19.3 us -> 11.7 us
    dot_general x13 -> x3, matrix products: 162 us -> 3.03 us  [the longest x1 1.45 us: shards(): slab = jnp.dot(placement, received, preferred_element_type=f32)]
    pallas_call x0 -> x2, Pallas kernels: none -> 103 us  [the longest x1 70.2 us: shards(): pl.pallas_call(score_kernel, out_shape=(jax.ShapeDtypeStruct((BASES * KO,...]
    psum x1 -> x0, waiting for transfers between devices: 100 us -> none  [shards(): summed = lax.psum(flat.astype(jnp.bfloat16), 'dom')]
    div x20 -> x0, other arithmetic: 88.5 us -> none  [the longest x1 87.1 us: shards(): factor = contrast / noise_var[None]]
    reduce_sum x10 -> x1, other arithmetic: 45.9 us -> 0.63 us  [shards(): jnp.sum((owners[:, :, None] == owners[:, None, :]) & earlier[None], axis=2)]
    convert_element_type x24 -> x1, other arithmetic: 39.3 us -> 0.23 us  [shards(): inserted = inserted.astype(bf16).reshape(half_lines, CL * WIDE)]
    another operation x2 -> x0, other arithmetic: 25.3 us -> none
    cos x9 -> x0, other arithmetic: 16.9 us -> none  [shift_waves(): return (jnp.cos(phases), jnp.sin(phases))]
  transfers between devices with their start and end apart: 3 -> 2, of which waited for: 2 -> 2; matrix products, arithmetic and copies ran while one was open for 24% -> 0% of each run, Pallas kernels for 0% -> 0%
where the time goes in v1:
time: 180 us; the launch traced here: 177 us
  Pallas kernels  103 us (57%)
  waiting for transfers between devices  38.7 us (22%)
  between operations  14.2 us (8%)
  local copies, waits for them, and re-layouts  11.7 us (6%)
  starting transfers between devices  4.53 us (3%)
  matrix products  3.03 us (2%)
    pallas_call x1, Pallas kernels, shards(): pl.pallas_call(score_kernel, out_shape=(jax.ShapeDtypeStruct((BASES * KO,...  70.2 us
    pallas_call x1, Pallas kernels, shards(): pl.pallas_call(back_kernel, out_shape=jax.ShapeDtypeStruct((CHUNKS * ROWS...  33.3 us
    reduce_scatter x1, waiting for transfers between devices, shards(): lax.psum_scatter(slab, 'orient', scatter_dimension=0, tiled=True)  30.1 us
    all_to_all x1, waiting for transfers between devices, shards(): received = lax.all_to_all(outgoing, 'dom', 0, 0, tiled=True)  8.59 us
    unnamed x20, local copies, waits for them, and re-layouts  7.07 us
    all_to_all x1, starting transfers between devices, shards(): received = lax.all_to_all(outgoing, 'dom', 0, 0, tiled=True)  4.49 us
  transfers between devices with their start and end apart: 2, of which 2 were waited for; matrix products, arithmetic and copies ran while one was open for 0% of the time, Pallas kernels for 0%

profile of v1, /device:TPU:1, one launch (start us, length us, event | category | flops | bytes accessed | tf_op | source)
XLA Modules:
  0.0 176.9 jit_solution(10262186462339732243)
XLA Ops:
  7.2 1.2 copy.22
  8.5 0.8 broadcast_in_dim.65.focus_ref
  9.2 0.7 broadcast_in_dim.66.label_ref
  9.9 0.9 copy-done.1
  10.9 0.9 copy-done.3
  11.8 0.8 copy-done.4
  12.6 0.7 copy-done.5
  13.3 0.7 copy-done.6
  14.0 0.7 copy-done.7
  14.7 70.2 %shard_map.158 = (bf16[288,192]{1,0:T(8,128)(2,1)S(1)}, f32[1,192]{1,0:T(1,128)S(1)}, bf16[16,192,4096]{2,1,0:T(8,128)(2,1)}) custom-call(bf16[16,32,256]{2,1,0:T(8,128)(2,1)S(1)} %reshape.76.refs_ref, bf16[192,256,256]{2,1,0:T(8,128)(2,1)} %images_hbm.1, f32[192,128]{1,0:T(8,128)S(1)} %broadcast_in_dim.65.focus_ref, f32[16,16,128]{2,1,0:T(8,128)S(1)} %bitcast.48, ...), custom_call_target="tpu_custom_call" | custom-call | tf_op jit(solution)/shard_map/pallas_call | solution.py:517
  85.0 33.3 %shard_map.159 = bf16[512,256]{1,0:T(8,128)(2,1)S(1)} custom-call(bf16[288,192]{1,0:T(8,128)(2,1)S(1)} %get-tuple-element.5.post_ref, bf16[16,192,4096]{2,1,0:T(8,128)(2,1)} %get-tuple-element.6.weighted_hbm, f32[8,128]{1,0:T(8,128)S(1)} %copy-done.6, f32[16,32,128]{2,1,0:T(8,128)S(1)} %copy-done.2), custom_call_target="tpu_custom_call" | custom-call | tf_op jit(solution)/shard_map/pallas_call | solution.py:555
  118.3 0.5 convolution_bitcast_fusion
  118.9 0.7 constant_dynamic-slice_fusion.1
  119.7 0.7 constant_dynamic-slice_fusion.5
  120.4 0.6 convert_reduce_fusion
  121.0 0.2 fusion.3
  121.3 1.1 convolution_convert_fusion.1
  122.4 4.5 %all-to-all-start = ((bf16[16,16,1024]{2,1,0:T(8,128)(2,1)}), bf16[16,16,1024]{2,1,0:T(8,128)(2,1)S(1)}, u32[]{:S(2)}, u32[]{:S(2)}) async-start(bf16[16,16,1024]{2,1,0:T(8,128)(2,1)} %bitcast.17), calls=%async_computation | async-start | bytes 1048576 | tf_op jit(solution)/shard_map/all_to_all | solution.py:599
  126.9 0.3 select_reduce_fusion
  127.4 8.6 %all-to-all-done = bf16[16,16,1024]{2,1,0:T(8,128)(2,1)S(1)} async-done(((bf16[16,16,1024]{2,1,0:T(8,128)(2,1)}), bf16[16,16,1024]{2,1,0:T(8,128)(2,1)S(1)}, u32[]{:S(2)}, u32[]{:S(2)}) %all-to-all-start) | async-done | bytes 524320 | tf_op jit(solution)/shard_map/all_to_all | solution.py:599
  136.2 1.5 convolution_convert_fusion
  137.6 30.1 %reduce-scatter.2.cloned.1.call-done = bf16[64,4,256]{2,0,1:T(8,128)(2,1)} async-done(((bf16[512,4,256]{2,0,1:T(8,128)(2,1)}), bf16[64,4,256]{2,0,1:T(8,128)(2,1)}) %reduce-scatter.2.cloned.1.call-update) | async-done | bytes 131088 | tf_op jit(solution)/shard_map/reduce_scatter | solution.py:605
  167.8 1.7 copy.26
  169.5 0.6 copy.35
  (25 shorter events, 0.6 us)
Async XLA Ops:
  7.2 111.2 %copy-start = (bf16[4,128,128]{2,1,0:T(8,128)(2,1)S(1)}, bf16[4,128,128]{2,1,0:T(8,128)(2,1)}, u32[]{:S(2)}) copy-start(bf16[4,128,128]{2,1,0:T(8,128)(2,1)} %param.24) | copy-start | bytes 393220
  7.2 77.8 %copy-start.2 = (f32[16,32,128]{2,1,0:T(8,128)S(1)}, f32[16,32,128]{2,1,0:T(8,128)}, u32[]{:S(2)}) copy-start(f32[16,32,128]{2,1,0:T(8,128)} %constant.45.clone.lines_ref) | copy-start | bytes 786436
  9.9 0.9 copy-start.1
  10.9 0.9 copy-start.3
  11.8 0.8 copy-start.4
  12.6 0.7 copy-start.5
  13.3 0.7 copy-start.6
  14.0 0.7 copy-start.7
  14.7 105.6 %copy-start.8 = (pred[128,128]{1,0:T(32,128)(4,1)S(1)}, pred[128,128]{1,0:T(32,128)(4,1)}, u32[]{:S(2)}) copy-start(pred[128,128]{1,0:T(32,128)(4,1)} %constant.47) | copy-start | bytes 49156
  122.4 13.6 %all-to-all-start = ((bf16[16,16,1024]{2,1,0:T(8,128)(2,1)}), bf16[16,16,1024]{2,1,0:T(8,128)(2,1)S(1)}, u32[]{:S(2)}, u32[]{:S(2)}) async-start(bf16[16,16,1024]{2,1,0:T(8,128)(2,1)} %bitcast.17), calls=%async_computation | async-start | bytes 1048576 | tf_op jit(solution)/shard_map/all_to_all | solution.py:599
  126.8 40.9 %reduce-scatter.2.cloned.1.call-start = ((), (), s32[]{:S(2)}) async-start(), calls=%async_computation.2 | async-start | bytes 1179648 | tf_op jit(solution)/shard_map/reduce_scatter | solution.py:605
Sparse Core Ops, SparseCore 0:
  137.7 29.9 reduce-scatter.1

commit v2 on v1

--- a/solution.py
+++ b/solution.py
@@ -243,7 +243,7 @@
                     sbuf[at : at + KO, j * WIDE + COLS : (j + 1) * WIDE] = m2.astype(bf16)
         nt = (((1,), (1,)), ((), ()))
         acc[...] += lax.dot_general(sbuf[...], wbuf[slot], nt, preferred_element_type=f32)
-        eacc[...] += lax.dot_general(rbuf[...], cbuf[...], nt, preferred_element_type=f32)
+        eacc[...] += lax.dot_general(cbuf[...], rbuf[...], nt, preferred_element_type=f32)
         return carry
 
     lax.fori_loop(0, NP, one_share, 0)
@@ -257,7 +257,7 @@
     for j in range(list_ref.shape[0]):
         hits = jnp.where(list_ref[j : j + 1, :] == wanted, 1.0, hits)
     usable = hits > 0.5
-    base = jnp.where(label_ref[0:1, :] == row % CL, prior_hit, prior_miss) - 0.5 * eacc[...]
+    base = jnp.where(label_ref[0:1, :] == row % CL, prior_hit, prior_miss) - 0.5 * jnp.transpose(eacc[...])
     xs = [[band(acc, a * 3 + b) for b in range(3)] for a in range(3)]
     peak = jnp.full((KO, N), excluded, f32)
     for t in range(BASES):
@@ -318,17 +318,18 @@
         stat_copy(k, group, (group + k) % GROUPS).wait_send()
 
 
-CHUNKS = 4
-ROWS = 32 * CL
+CHUNKS = 8
+ROWS = PL * CL
 HALF = ROWS // 2
 QUART = ROWS // 4
 
 
 def back_kernel(
-    post_ref, weighted_hbm, coltab_ref, lines_ref,
+    post_ref, weighted_hbm, coltab_ref, lines_ref, owner_ref, slab_ref, kernel_ref, interp_ref,
     out_ref,
     wbuf, part, r1, r2, p2, q1, q2,
-    in_sem, send_sem, recv_sem,
+    rowre, rowim, mapped, outgoing, received, placer, sender, slab, sib, chip, y1, y2,
+    in_sem, send_sem, recv_sem, xsend, xrecv, ysend, yrecv,
 ):
     dom = lax.axis_index("dom")
     group = lax.axis_index("orient")
@@ -338,25 +339,28 @@
         return z * SIDE + (x + d) % SIDE if axis == "x" else ((z + d) % SIDE) * SIDE + x
 
     def share_of(i):
-        return 2 * (i // 4) + i % 2 + 8 * ((i % 4) // 2)
+        return i // 2 + CHUNKS * (i % 2)
 
     def load(i):
         return pltpu.make_async_copy(weighted_hbm.at[share_of(i)], wbuf.at[i % 3], in_sem.at[i % 3])
 
     load(0).start()
     load(1).start()
+    core, high = group % 2, group // 2
+    sibling = high * 2 + 1 - core
     barrier = pltpu.get_barrier_semaphore()
-    for axis in ("x", "z"):
-        for d in (1, 3):
-            pl.semaphore_signal(barrier, inc=1, device_id=(neighbour(axis, d), group), device_id_type=MESH)
-    pl.semaphore_wait(barrier, 4)
+    for k in range(1, NP):
+        pl.semaphore_signal(barrier, inc=1, device_id=((dom + k) % NP, group), device_id_type=MESH)
+    for to in (sibling, (group + 2) % GROUPS, (group + 6) % GROUPS):
+        pl.semaphore_signal(barrier, inc=1, device_id=(dom, to), device_id_type=MESH)
+    pl.semaphore_wait(barrier, NP + 2)
 
     ca, sa = coltab_ref[1:2, :], coltab_ref[2:3, :]
 
     def compute(i):
         load(i).wait()
         pl.when(i + 2 < NP)(lambda: load(i + 2).start())
-        chunk, half, share = i // 4, (i % 4) // 2, share_of(i)
+        chunk, half, share = i // 2, i % 2, share_of(i)
         for four in range(PL // 4):
             outs = []
             for j in range(four * 4, four * 4 + 4):
@@ -382,10 +386,9 @@
                         axis=1,
                     )
                 )
-            row = pl.multiple_of((i % 2) * (PL * CL) + four * 16, 16)
             for o in range(OG):
                 piece = jnp.concatenate([v[o * CL : (o + 1) * CL, :] for v in outs], axis=0)
-                part[chunk, o // 2, (o % 2) * 2 + half, pl.ds(row, 16), :] = piece.astype(bf16)
+                part[chunk, o // 2, (o % 2) * 2 + half, pl.ds(four * 16, 16), :] = piece.astype(bf16)
 
     def setup(h):
         first, second = ("x", "z") if h == 0 else ("z", "x")
@@ -455,31 +458,140 @@
                     p2[c, h, to, rows, :] = new.astype(bf16)
             elif stage == 4:
                 new = p2[c, h, s].astype(f32) + q2[c, h, 0].astype(f32) + q2[c, h, 1].astype(f32)
-                out_ref[pl.ds(pl.multiple_of(c * ROWS, ROWS) + h * HALF, HALF), :] = new.astype(bf16)
+                new = new.astype(bf16).astype(f32)
+                rows = pl.ds(pl.multiple_of(c * ROWS, ROWS) + h * HALF, HALF)
+                rowre[rows, :] = new[:, :COLS]
+                rowim[rows, :] = new[:, COLS:]
             if stage < 4:
                 for cp_ in copies(c, h, stage):
                     cp_.start()
+
+    def ranks(own):
+        hot = own == lax.broadcasted_iota(jnp.int32, (NP, COLS), 0)
+        before = lax.broadcasted_iota(jnp.int32, (COLS, COLS), 0) < lax.broadcasted_iota(
+            jnp.int32, (COLS, COLS), 1
+        )
+        hot = jnp.where(hot, 1.0, 0.0)
+        counts = jnp.dot(
+            hot.astype(bf16), jnp.where(before, 1.0, 0.0).astype(bf16), preferred_element_type=f32
+        )
+        return jnp.sum(hot * counts, axis=0, keepdims=True).astype(jnp.int32)
+
+    def prepare():
+        slot_row = lax.broadcasted_iota(jnp.int32, (CAP, COLS), 0)
+        mine = pl.ds(pl.multiple_of(group * OG, OG), OG)
+        owners, slabs, kernels = owner_ref[mine, :], slab_ref[mine, :].astype(f32), kernel_ref[mine, :]
+
+        def block(a, b):
+            return a[b // 2 : b // 2 + 1, (b % 2) * COLS : (b % 2 + 1) * COLS]
+
+        def own_block(a):
+            a = jnp.where(dom % 2 == 0, a[:, :COLS], a[:, COLS:]).astype(f32)
+            row = lax.broadcasted_iota(jnp.int32, (OG, COLS), 0)
+            return jnp.sum(jnp.where(row == dom // 2, a, 0.0), axis=0, keepdims=True).astype(jnp.int32)
+
+        for b in range(NP):
+            own = block(owners, b)
+            live = (own == dom) & (ranks(own) == slot_row)
+            target = jnp.sum(jnp.where(live, block(slabs, b) + 1.0, 0.0), axis=1, keepdims=True)
+            spot = lax.broadcasted_iota(jnp.int32, (CAP, SLAB_ROWS), 1).astype(f32) + 1.0
+            placer[b * CAP : (b + 1) * CAP, :] = jnp.where(target == spot, 1.0, 0.0)
+        own = own_block(owners)
+        slot = own * CAP + ranks(own)
+        hit = slot == lax.broadcasted_iota(jnp.int32, (NP * CAP, COLS), 0)
+        kern = own_block(kernels)
+        for w in range(4):
+            sender[:, w * COLS : (w + 1) * COLS] = jnp.where(hit & (kern == w), 1.0, 0.0).astype(bf16)
 
     def tick(t, carry):
         @pl.when(t < CHUNKS)
         def _():
             def body(q, c):
-                compute(t * 4 + q)
+                compute(t * 2 + q)
                 return c
 
-            lax.fori_loop(0, 4, body, 0)
-
+            lax.fori_loop(0, 2, body, 0)
+
+        pl.when(t == CHUNKS)(prepare)
         for stage in range(5):
             c = t - stage
             pl.when((c >= 0) & (c < CHUNKS))(functools.partial(advance, c, stage))
         return carry
 
     lax.fori_loop(0, CHUNKS + 4, tick, 0)
+
+    for k in range(CL):
+        for n_, ref in enumerate((rowre, rowim)):
+            rows = ref[pl.ds(k, COLS, stride=CL), :].astype(bf16)
+            for w in range(4):
+                new = jnp.dot(rows, interp_ref[w], preferred_element_type=f32)
+                at = (2 * k + n_) * COLS
+                mapped[w * COLS : (w + 1) * COLS, at : at + COLS] = new.astype(bf16)
+    rows = jnp.dot(sender[...], mapped[...], preferred_element_type=f32)
+    outgoing[...] = rows.astype(bf16).reshape(NP, CAP, CL * WIDE)
+
+    def to_owner(k, src, dst, dev):
+        return pltpu.make_async_remote_copy(
+            src_ref=src, dst_ref=dst, send_sem=xsend.at[k], recv_sem=xrecv.at[k],
+            device_id=(dev, group), device_id_type=MESH,
+        )
+
+    for k in range(1, NP):
+        to = (dom + k) % NP
+        to_owner(k, outgoing.at[to], received.at[dom], to).start()
+    received[dom] = outgoing[dom]
+    place = jnp.transpose(placer[...]).astype(bf16)
+    for k in range(1, NP):
+        frm = (dom + NP - k) % NP
+        to_owner(k, outgoing.at[frm], received.at[frm], frm).wait_recv()
+    rows = jnp.dot(place, received[...].reshape(NP * CAP, CL * WIDE), preferred_element_type=f32)
+    slab[...] = rows.astype(bf16).reshape(SIDE, 2, SLAB_ROWS // GROUPS, CL * WIDE)
+
+    def over_orient(i, src, dst, dev):
+        return pltpu.make_async_remote_copy(
+            src_ref=src, dst_ref=dst, send_sem=ysend.at[i], recv_sem=yrecv.at[i],
+            device_id=(dom, dev), device_id_type=MESH,
+        )
+
+    swap = over_orient(0, slab.at[:, 1 - core], sib, sibling)
+    swap.start()
+    swap.wait_recv()
+    part_rows = SLAB_ROWS // GROUPS // 2
+    sides = ((6, 3), (2, 1))
+    far = (high + 2) % SIDE
+    chip[far] = (slab[far, core].astype(f32) + sib[far].astype(f32)).astype(bf16)
+    first = [
+        over_orient(1 + n_, chip.at[far, pl.ds(n_ * part_rows, part_rows)], y1.at[n_], (group + d) % GROUPS)
+        for n_, (d, _) in enumerate(sides)
+    ]
+    for c in first:
+        c.start()
+    for d in (3, 1, 0):
+        to = (high + d) % SIDE
+        chip[to] = (slab[to, core].astype(f32) + sib[to].astype(f32)).astype(bf16)
+    second = []
+    for n_, (d, dy) in enumerate(sides):
+        to = (high + dy) % SIDE
+        first[n_].wait_recv()
+        rows = pl.ds(n_ * part_rows, part_rows)
+        chip[to, rows] = (chip[to, rows].astype(f32) + y1[n_].astype(f32)).astype(bf16)
+        c = over_orient(3 + n_, chip.at[to], y2.at[n_], (group + d) % GROUPS)
+        c.start()
+        second.append(c)
+    for c in second:
+        c.wait_recv()
+    out_ref[...] = chip[high].astype(f32) + y2[0].astype(f32) + y2[1].astype(f32)
+
     for c in range(CHUNKS):
         for h in (0, 1):
             for stage in range(4):
                 for cp_ in copies(c, h, stage):
                     cp_.wait_send()
+    for k in range(1, NP):
+        to = (dom + k) % NP
+        to_owner(k, outgoing.at[to], received.at[dom], to).wait_send()
+    for c in (swap, *first, *second):
+        c.wait_send()
 
 
 VM = pl.BlockSpec(memory_space=pltpu.VMEM)
@@ -533,7 +645,7 @@
             pltpu.VMEM((BASES * KO, PK), bf16),
             pltpu.VMEM((KO, PL * COLS), bf16),
             pltpu.VMEM((BASES * KO, N), f32),
-            pltpu.VMEM((KO, N), f32),
+            pltpu.VMEM((N, KO), f32),
             pltpu.VMEM((N, COLS), f32),
             pltpu.VMEM((N, COLS), f32),
             pltpu.VMEM((N, COLS), f32),
@@ -552,10 +664,11 @@
     )(
         refs, images, focus, noise_var.reshape(NP, PL, COLS), orient_list.T, labels, rowtab, offs, coltab, lines
     )
-    block = pl.pallas_call(
+    piece = SLAB_ROWS // GROUPS
+    volume = pl.pallas_call(
         back_kernel,
-        out_shape=jax.ShapeDtypeStruct((CHUNKS * ROWS, WIDE), bf16),
-        in_specs=[VM, ANY, VM, VM],
+        out_shape=jax.ShapeDtypeStruct((piece, CL * WIDE), f32),
+        in_specs=[VM, ANY] + [VM] * 6,
         out_specs=VM,
         scratch_shapes=[
             pltpu.VMEM((3, N, PK), bf16),
@@ -565,45 +678,31 @@
             pltpu.VMEM((CHUNKS, 2, SIDE, HALF, WIDE), bf16),
             pltpu.VMEM((CHUNKS, 2, 2, QUART, WIDE), bf16),
             pltpu.VMEM((CHUNKS, 2, 2, HALF, WIDE), bf16),
+            pltpu.VMEM((CHUNKS * ROWS, COLS), f32),
+            pltpu.VMEM((CHUNKS * ROWS, COLS), f32),
+            pltpu.VMEM((4 * COLS, CL * WIDE), bf16),
+            pltpu.VMEM((NP, CAP, CL * WIDE), bf16),
+            pltpu.VMEM((NP, CAP, CL * WIDE), bf16),
+            pltpu.VMEM((NP * CAP, SLAB_ROWS), f32),
+            pltpu.VMEM((NP * CAP, 4 * COLS), bf16),
+            pltpu.VMEM((SIDE, 2, piece, CL * WIDE), bf16),
+            pltpu.VMEM((SIDE, piece, CL * WIDE), bf16),
+            pltpu.VMEM((SIDE, piece, CL * WIDE), bf16),
+            pltpu.VMEM((2, piece // 2, CL * WIDE), bf16),
+            pltpu.VMEM((2, piece, CL * WIDE), bf16),
             pltpu.SemaphoreType.DMA((3,)),
             pltpu.SemaphoreType.DMA((CHUNKS, 16)),
             pltpu.SemaphoreType.DMA((CHUNKS, 16)),
+            pltpu.SemaphoreType.DMA((NP,)),
+            pltpu.SemaphoreType.DMA((NP,)),
+            pltpu.SemaphoreType.DMA((5,)),
+            pltpu.SemaphoreType.DMA((5,)),
         ],
         compiler_params=pltpu.CompilerParams(
             collective_id=1, has_side_effects=True, vmem_limit_bytes=40 * 2**20
         ),
-    )(post, weighted, coltab, lines)
-
-    group = lax.axis_index("orient")
-    dom = lax.axis_index("dom")
-    half_lines = LINES // 2
-
-    def group_rows(a):
-        return lax.dynamic_slice_in_dim(a, group * OG, OG, 0).reshape(NP, half_lines)
-
-    owners, slabs, kernels = group_rows(owner[:, :, 0]), group_rows(slab_row), group_rows(kernel_index)
-    mine = lax.dynamic_slice_in_dim(kernels, dom, 1, 0)[0]
-    rows = block.reshape(half_lines, CL * 2, COLS)
-    every = jnp.einsum("rxc,wcd->rwxd", rows, interp, preferred_element_type=f32)
-    inserted = jnp.zeros(rows.shape, f32)
-    for w in range(interp.shape[0]):
-        inserted = jnp.where((mine == w)[:, None, None], every[:, w], inserted)
-    inserted = inserted.astype(bf16).reshape(half_lines, CL * WIDE)
-    earlier = np.tril(np.ones((half_lines, half_lines), bool), -1)
-    rank = jnp.sum((owners[:, :, None] == owners[:, None, :]) & earlier[None], axis=2).astype(jnp.int32)
-    own_mine = lax.dynamic_slice_in_dim(owners, dom, 1, 0)[0]
-    rank_mine = lax.dynamic_slice_in_dim(rank, dom, 1, 0)[0]
-    slot_ids = jnp.arange(NP * CAP)
-    sendmap = ((own_mine * CAP + rank_mine)[None, :] == slot_ids[:, None]).astype(bf16)
-    outgoing = jnp.dot(sendmap, inserted, preferred_element_type=f32).astype(bf16)
-    received = lax.all_to_all(outgoing, "dom", 0, 0, tiled=True)
-    live = (owners[:, None, :] == dom) & (rank[:, None, :] == jnp.arange(CAP)[None, :, None])
-    target = jnp.max(jnp.where(live, slabs[:, None, :], -1), axis=2).reshape(-1)
-    placement = (target[None, :] == jnp.arange(SLAB_ROWS)[:, None]).astype(bf16)
-    slab = jnp.dot(placement, received, preferred_element_type=f32)
-    slab = slab.reshape(SLAB_ROWS, CL, WIDE).astype(bf16)
-    volume = lax.psum_scatter(slab, "orient", scatter_dimension=0, tiled=True).astype(f32)
-    return volume, evidence.reshape(N)
+    )(post, weighted, coltab, lines, owner[:, :, 0], slab_row, kernel_index, interp)
+    return volume.reshape(piece, CL, WIDE), evidence.reshape(N)
 
 
 def solution(mesh):

time: 180 us -> 143 us (0.79); the launches traced: 177 us -> 143 us
  waiting for transfers between devices: 38.7 us -> 0 us
  Pallas kernels: 103 us -> 133 us
  between operations: 14.2 us -> 0.76 us
  starting transfers between devices: 4.53 us -> 0 us
  matrix products: 3.03 us -> 0 us
  local copies, waits for them, and re-layouts: 11.7 us -> 8.92 us
    reduce_scatter x1 -> x0, waiting for transfers between devices: 30.1 us -> none  [shards(): lax.psum_scatter(slab, 'orient', scatter_dimension=0, tiled=True)]
    pallas_call x1, Pallas kernels: 33.3 us -> 63.4 us  [shards(): pl.pallas_call(back_kernel, out_shape=jax.ShapeDtypeStruct((piece, CL * W...]
    all_to_all x1 -> x0, waiting for transfers between devices: 8.59 us -> none  [shards(): received = lax.all_to_all(outgoing, 'dom', 0, 0, tiled=True)]
    all_to_all x1 -> x0, starting transfers between devices: 4.49 us -> none  [shards(): received = lax.all_to_all(outgoing, 'dom', 0, 0, tiled=True)]
    dot_general x3 -> x0, matrix products: 3.03 us -> none  [the longest x1 1.45 us: shards(): slab = jnp.dot(placement, received, preferred_element_type=f32)]
    unnamed x20 -> x24, local copies, waits for them, and re-layouts: 7.07 us -> 5.37 us
  transfers between devices with their start and end apart: 2 -> 0, of which waited for: 2 -> 0; matrix products, arithmetic and copies ran while one was open for 0% -> 0% of each run, Pallas kernels for 0% -> 0%
where the time goes in v2:
time: 143 us
  Pallas kernels  133 us (93%)
  local copies, waits for them, and re-layouts  8.92 us (6%)
    pallas_call x1, Pallas kernels, shards(): pl.pallas_call(score_kernel, out_shape=(jax.ShapeDtypeStruct((BASES * KO,...  70.1 us
    pallas_call x1, Pallas kernels, shards(): pl.pallas_call(back_kernel, out_shape=jax.ShapeDtypeStruct((piece, CL * W...  63.4 us
    unnamed x24, local copies, waits for them, and re-layouts  5.37 us

profile of v2, /device:TPU:1, one launch (start us, length us, event | category | flops | bytes accessed | tf_op | source)
XLA Modules:
  0.0 143.1 jit_solution(14811207516559819398)
XLA Ops:
  0.6 0.0 copy-start.1
  0.6 0.0 copy-start.10
  0.7 0.0 copy-start.4
  0.7 0.0 copy-start.5
  0.7 0.0 copy-start.3
  0.7 1.2 copy.16
  1.9 0.1 reshape.18.refs_ref
  2.0 0.8 broadcast_in_dim.4.focus_ref
  2.7 0.7 broadcast_in_dim.5.label_ref
  3.4 0.9 copy-done
  4.4 0.9 copy-done.2
  5.3 0.8 copy-done.6
  6.1 0.7 copy-done.7
  6.8 0.7 copy-done.8
  7.5 0.7 copy-done.9
  8.2 70.1 %shard_map.149 = (bf16[288,192]{1,0:T(8,128)(2,1)S(1)}, f32[1,192]{1,0:T(1,128)S(1)}, bf16[16,192,4096]{2,1,0:T(8,128)(2,1)}) custom-call(bf16[16,32,256]{2,1,0:T(8,128)(2,1)S(1)} %reshape.18.refs_ref, bf16[192,256,256]{2,1,0:T(8,128)(2,1)} %images_hbm.1, f32[192,128]{1,0:T(8,128)S(1)} %broadcast_in_dim.4.focus_ref, f32[16,16,128]{2,1,0:T(8,128)S(1)} %bitcast.8, ...), custom_call_target="tpu_custom_call" | custom-call | tf_op jit(solution)/shard_map/pallas_call | solution.py:629
  78.3 0.0 copy-done.10
  78.3 0.0 copy-done.1
  78.3 0.0 copy-done.4
  78.3 0.0 copy-done.5
  78.3 0.0 copy-done.3
  78.4 63.4 %shard_map.150 = f32[64,1024]{1,0:T(8,128)S(1)} custom-call(bf16[288,192]{1,0:T(8,128)(2,1)S(1)} %get-tuple-element.5.post_ref, bf16[16,192,4096]{2,1,0:T(8,128)(2,1)} %get-tuple-element.6.weighted_hbm, f32[8,128]{1,0:T(8,128)S(1)} %copy-done.8, f32[16,32,128]{2,1,0:T(8,128)S(1)} %copy-done.1, s32[64,256]{1,0:T(8,128)S(1)} %bitcast.7, ...), custom_call_target="tpu_custom_call" | custom-call | tf_op jit(solution)/shard_map/pallas_call | solution.py:668
  141.7 0.8 reshape.20
  142.5 0.6 copy.21
  (7 shorter events, 0.0 us)
Async XLA Ops:
  0.6 77.7 %copy-start.1 = (f32[16,32,128]{2,1,0:T(8,128)S(1)}, f32[16,32,128]{2,1,0:T(8,128)}, u32[]{:S(2)}) copy-start(f32[16,32,128]{2,1,0:T(8,128)} %constant.11.clone.lines_ref) | copy-start | bytes 786436
  0.6 77.6 %copy-start.10 = (s32[64,256,1]{1,2,0:T(1,128)S(1)}, s32[64,256,1]{1,2,0:T(1,128)}, u32[]{:S(2)}) copy-start(s32[64,256,1]{1,2,0:T(1,128)} %param.20) | copy-start | bytes 196612
  0.7 77.7 %copy-start.4 = (s32[64,256]{1,0:T(8,128)S(1)}, s32[64,256]{1,0:T(8,128)}, u32[]{:S(2)}) copy-start(s32[64,256]{1,0:T(8,128)} %slab_ref.1) | copy-start | bytes 196612
  0.7 77.7 %copy-start.5 = (s32[64,256]{1,0:T(8,128)S(1)}, s32[64,256]{1,0:T(8,128)}, u32[]{:S(2)}) copy-start(s32[64,256]{1,0:T(8,128)} %kernel_ref.1) | copy-start | bytes 196612
  0.7 77.7 %copy-start.3 = (bf16[4,128,128]{2,1,0:T(8,128)(2,1)S(1)}, bf16[4,128,128]{2,1,0:T(8,128)(2,1)}, u32[]{:S(2)}) copy-start(bf16[4,128,128]{2,1,0:T(8,128)(2,1)} %interp_ref.1) | copy-start | bytes 393220
  3.4 0.9 copy-start
  4.4 0.9 copy-start.2
  5.3 0.8 copy-start.6
  6.1 0.7 copy-start.7
  6.8 0.7 copy-start.8
  7.5 0.7 copy-start.9

commit v3 on v2

--- a/solution.py
+++ b/solution.py
@@ -23,6 +23,7 @@
 SIDE = 4
 GROUPS = 8
 BASES = 9
+SHARED = N // 2
 CAP = 16
 
 prior_hit = math.log(0.55)
@@ -115,6 +116,23 @@
     return s * (1.0 - 2.0 * odd)
 
 
+def column_waves():
+    ang = lax.broadcasted_iota(jnp.int32, (1, COLS), 1).astype(f32) * (math.pi / COLS)
+    return fine_sin(ang + math.pi / 2), fine_sin(ang)
+
+
+def line_waves(share):
+    row = lax.broadcasted_iota(jnp.int32, (2 * PL, COLS), 0)
+    line = (share * PL - LINES // 2 + row % PL).astype(f32)
+    return fine_sin(line * (2 * math.pi / LINES) + jnp.where(row < PL, math.pi / 2, 0.0))
+
+
+def line_angles(share):
+    lane = lax.broadcasted_iota(jnp.int32, (1, COLS), 1)
+    line = (share * PL - LINES // 2 + lane % PL).astype(f32) * (2.0 / LINES)
+    return line * line, jnp.where(lane < PL, 0.3, 0.3 + math.pi / 2)
+
+
 def pick(step, values):
     out = jnp.int32(0)
     for i, v in enumerate(values):
@@ -124,14 +142,18 @@
 
 
 def score_kernel(
-    refs_ref, images_hbm, focus_ref, noise_ref, list_ref, label_ref, rowtab_ref, offs_ref, coltab_ref, lines_ref,
+    refs_ref, images_hbm, focus_ref, noise_ref, list_ref, label_ref,
     post_ref, evid_ref, weighted_hbm,
-    refs_all, ibuf, fre, fim, wbuf, cbuf, sbuf, rbuf, acc, eacc, colsin, colcos, angtab, sc, stats,
-    send_sem, recv_sem, ssend_sem, srecv_sem, in_sem, out_sem,
+    refs_all, ibuf, fre, fim, wall, call, sbuf, rbuf, acc, eacc, focus, colsin, colcos, angtab, waves, sc, stats,
+    send_sem, recv_sem, ssend_sem, srecv_sem, in_sem, out_sem, wsend, wrecv, csend, crecv,
 ):
     dom = lax.axis_index("dom")
     group = lax.axis_index("orient")
     z, x = dom // SIDE, dom % SIDE
+    core = group % 2
+    sibling = group + 1 - 2 * core
+    mine = pl.ds(pl.multiple_of(core * SHARED, SHARED), SHARED)
+    theirs = pl.ds(pl.multiple_of((1 - core) * SHARED, SHARED), SHARED)
 
     def origin(dz, dx):
         return ((z + dz) % SIDE) * SIDE + (x + dx) % SIDE
@@ -141,10 +163,20 @@
 
     def image_copy(step):
         lines = pl.ds(pl.multiple_of(step_origin(step) * PL, PL), PL)
-        return pltpu.make_async_copy(images_hbm.at[:, lines, :], ibuf.at[step % 2], in_sem.at[step % 2])
+        return pltpu.make_async_copy(images_hbm.at[mine, lines, :], ibuf.at[step % 2], in_sem.at[step % 2])
 
     def weighted_copy(step):
-        return pltpu.make_async_copy(wbuf.at[step % 2], weighted_hbm.at[step_origin(step)], out_sem.at[step % 2])
+        return pltpu.make_async_copy(wall.at[step], weighted_hbm.at[step_origin(step)], out_sem.at[step])
+
+    def swap(step, rows):
+        def one(buf, send, recv):
+            part = buf.at[step, rows]
+            return pltpu.make_async_remote_copy(
+                src_ref=part, dst_ref=part, send_sem=send.at[step], recv_sem=recv.at[step],
+                device_id=(dom, sibling), device_id_type=MESH,
+            )
+
+        return one(wall, wsend, wrecv), one(call, csend, crecv)
 
     image_copy(0).start()
 
@@ -185,21 +217,21 @@
 
     traffic(STEPS[0])
     refs_all[dom] = refs_ref[...]
-    focus = focus_ref[...]
-    colang = focus[:, 0:1] * coltab_ref[0:1, :]
+    wide = jnp.transpose(jnp.broadcast_to(focus_ref[...], (COLS, N)))
+    focus[...] = jnp.where(core == 0, wide[:SHARED, :], wide[SHARED:, :])
+    col = lax.broadcasted_iota(jnp.int32, (1, COLS), 1).astype(f32) * (2.0 / LINES)
+    colang = focus[...] * (col * col)
     colsin[...] = fine_sin(colang)
     colcos[...] = fine_sin(colang + math.pi / 2)
     acc[...] = jnp.zeros_like(acc)
     eacc[...] = jnp.zeros_like(eacc)
 
-    def one_share(step, carry):
-        for i in range(1, NP):
-            if STEPS[i]:
-                pl.when(step == i)(functools.partial(traffic, STEPS[i]))
+    def weigh_share(step):
         share = step_origin(step)
         slot = step % 2
         pl.when(step + 1 < NP)(lambda: image_copy(step + 1).start())
-        angtab[...] = fine_sin(focus_ref[...] * rowtab_ref[share, 0:1, :] + offs_ref[0:1, :])
+        far, start = line_angles(share)
+        angtab[...] = fine_sin(focus[...] * far + start)
         image_copy(step).wait()
 
         def widen(i, c):
@@ -210,11 +242,11 @@
             fim[rows, :] = part[:, COLS:]
             return c
 
-        lax.fori_loop(0, N // 8, widen, 0)
-        pl.when(step >= 2)(lambda: weighted_copy(step - 2).wait())
+        lax.fori_loop(0, SHARED // 8, widen, 0)
 
         def weigh(i, c):
             rows = pl.ds(pl.multiple_of(i * 32, 32), 32)
+            to = pl.ds(pl.multiple_of(core * SHARED + i * 32, 32), 32)
             cs, cc = colsin[rows, :], colcos[rows, :]
             ang = angtab[rows, :]
             for j in range(PL):
@@ -222,19 +254,29 @@
                 con = ang[:, j : j + 1] * cc + ang[:, PL + j : PL + j + 1] * cs
                 fac = con * inv
                 take = pl.ds(i * (32 * PL) + j, 32, stride=PL)
-                wbuf[slot, rows, j * WIDE : j * WIDE + COLS] = (fre[take, :] * fac).astype(bf16)
-                wbuf[slot, rows, j * WIDE + COLS : (j + 1) * WIDE] = (fim[take, :] * fac).astype(bf16)
-                cbuf[rows, j * COLS : (j + 1) * COLS] = (con * fac).astype(bf16)
+                wall[step, to, j * WIDE : j * WIDE + COLS] = (fre[take, :] * fac).astype(bf16)
+                wall[step, to, j * WIDE + COLS : (j + 1) * WIDE] = (fim[take, :] * fac).astype(bf16)
+                call[step, to, j * COLS : (j + 1) * COLS] = (con * fac).astype(bf16)
             return c
 
-        lax.fori_loop(0, N // 32, weigh, 0)
-        weighted_copy(step).start()
-
-        ca, sa = coltab_ref[1:2, :], coltab_ref[2:3, :]
+        lax.fori_loop(0, SHARED // 32, weigh, 0)
+        for c in swap(step, mine):
+            c.start()
+
+    weigh_share(0)
+
+    def one_share(step, carry):
+        pl.when(step + 1 < NP)(lambda: weigh_share(step + 1))
+        for i in range(1, NP):
+            if STEPS[i]:
+                pl.when(step == i)(functools.partial(traffic, STEPS[i]))
+        share = step_origin(step)
+        waves[...] = line_waves(share)
+        ca, sa = column_waves()
         for j in range(PL):
             ref = refs_all[share, j].astype(f32)
             re, im = ref[:, :COLS], ref[:, COLS:]
-            cp, sp = lines_ref[share, j : j + 1, :], lines_ref[share, PL + j : PL + j + 1, :]
+            cp, sp = waves[j : j + 1, :], waves[PL + j : PL + j + 1, :]
             rbuf[:, j * COLS : (j + 1) * COLS] = (re * re + im * im).astype(bf16)
             for a, (r, m) in enumerate(((re, im), (re * ca, im * ca), (im * -sa, re * sa))):
                 for b, (r2, m2) in enumerate(((r, m), (r * cp, m * cp), (m * -sp, r * sp))):
@@ -242,8 +284,11 @@
                     sbuf[at : at + KO, j * WIDE : j * WIDE + COLS] = r2.astype(bf16)
                     sbuf[at : at + KO, j * WIDE + COLS : (j + 1) * WIDE] = m2.astype(bf16)
         nt = (((1,), (1,)), ((), ()))
-        acc[...] += lax.dot_general(sbuf[...], wbuf[slot], nt, preferred_element_type=f32)
-        eacc[...] += lax.dot_general(cbuf[...], rbuf[...], nt, preferred_element_type=f32)
+        for c in swap(step, theirs):
+            c.wait_recv()
+        weighted_copy(step).start()
+        acc[...] += lax.dot_general(sbuf[...], wall[step], nt, preferred_element_type=f32)
+        eacc[...] += lax.dot_general(call[step], rbuf[...], nt, preferred_element_type=f32)
         return carry
 
     lax.fori_loop(0, NP, one_share, 0)
@@ -310,8 +355,10 @@
         for a, v in enumerate((none, more + less, more - less)):
             post_ref[(a * 3 + b) * KO : (a * 3 + b + 1) * KO, :] = v.astype(bf16)
 
-    weighted_copy(NP - 2).wait()
-    weighted_copy(NP - 1).wait()
+    for i in range(NP):
+        weighted_copy(i).wait()
+        for c in swap(i, mine):
+            c.wait_send()
     for i in range(len(MSGS)):
         message(i).wait_send()
     for k in range(1, GROUPS):
@@ -319,16 +366,17 @@
 
 
 CHUNKS = 8
+LAG = 2
 ROWS = PL * CL
 HALF = ROWS // 2
 QUART = ROWS // 4
 
 
 def back_kernel(
-    post_ref, weighted_hbm, coltab_ref, lines_ref, owner_ref, slab_ref, kernel_ref, interp_ref,
+    post_ref, weighted_hbm, owner_ref, slab_ref, kernel_ref, interp_ref,
     out_ref,
     wbuf, part, r1, r2, p2, q1, q2,
-    rowre, rowim, mapped, outgoing, received, placer, sender, slab, sib, chip, y1, y2,
+    rowre, rowim, mapped, outgoing, received, placer, sender, slab, sib, chip, y1, y2, waves,
     in_sem, send_sem, recv_sem, xsend, xrecv, ysend, yrecv,
 ):
     dom = lax.axis_index("dom")
@@ -355,19 +403,20 @@
         pl.semaphore_signal(barrier, inc=1, device_id=(dom, to), device_id_type=MESH)
     pl.semaphore_wait(barrier, NP + 2)
 
-    ca, sa = coltab_ref[1:2, :], coltab_ref[2:3, :]
+    ca, sa = column_waves()
 
     def compute(i):
         load(i).wait()
         pl.when(i + 2 < NP)(lambda: load(i + 2).start())
-        chunk, half, share = i // 2, i % 2, share_of(i)
+        chunk, half = i // 2, i % 2
+        waves[...] = line_waves(share_of(i))
         for four in range(PL // 4):
             outs = []
             for j in range(four * 4, four * 4 + 4):
                 g = jnp.dot(
                     post_ref[...], wbuf[i % 3, :, j * WIDE : (j + 1) * WIDE], preferred_element_type=f32
                 )
-                cp, sp = lines_ref[share, j : j + 1, :], lines_ref[share, PL + j : PL + j + 1, :]
+                cp, sp = waves[j : j + 1, :], waves[PL + j : PL + j + 1, :]
                 vs = []
                 for a in range(3):
                     g0, gc, gs = (g[(a * 3 + b) * KO : (a * 3 + b + 1) * KO, :] for b in range(3))
@@ -514,11 +563,11 @@
 
         pl.when(t == CHUNKS)(prepare)
         for stage in range(5):
-            c = t - stage
+            c = t - LAG * stage
             pl.when((c >= 0) & (c < CHUNKS))(functools.partial(advance, c, stage))
         return carry
 
-    lax.fori_loop(0, CHUNKS + 4, tick, 0)
+    lax.fori_loop(0, CHUNKS + 4 * LAG, tick, 0)
 
     for k in range(CL):
         for n_, ref in enumerate((rowre, rowim)):
@@ -598,34 +647,10 @@
 ANY = pl.BlockSpec(memory_space=pl.ANY)
 
 
-def constants():
-    c = np.arange(COLS, dtype=np.float32)
-    l = np.arange(LINES, dtype=np.float32) - LINES // 2
-    half = float(LINES // 2)
-    coltab = np.zeros((8, COLS), np.float32)
-    coltab[0] = c * c / (half * half)
-    coltab[1] = np.cos(math.pi * c / COLS)
-    coltab[2] = np.sin(math.pi * c / COLS)
-    rowtab = np.zeros((NP, 8, COLS), np.float32)
-    rsq = (l * l / (half * half)).reshape(NP, 1, PL)
-    rowtab[:, :, :PL] = rsq
-    rowtab[:, :, PL : 2 * PL] = rsq
-    offs = np.zeros((8, COLS), np.float32)
-    offs[:, :PL] = 0.3
-    offs[:, PL : 2 * PL] = 0.3 + math.pi / 2
-    ang = (math.pi * l / half).reshape(NP, PL, 1)
-    lines = np.concatenate([np.cos(ang), np.sin(ang)], axis=1)
-    lines = np.broadcast_to(lines, (NP, 2 * PL, COLS)).astype(np.float32)
-    return coltab, rowtab, offs, lines
-
-
 def shards(
     images, defocus, noise_var, references, orient_list, class_label, owner, slab_row, kernel_index, interp
 ):
-    coltab, rowtab, offs, lines = (jnp.asarray(a) for a in constants())
     refs = jnp.transpose(references, (2, 1, 0, 3)).reshape(PL, KO, WIDE)
-    focus = jnp.broadcast_to(defocus[:, None], (N, COLS))
-    labels = jnp.broadcast_to(class_label[None, :], (8, N))
     post, evidence, weighted = pl.pallas_call(
         score_kernel,
         out_shape=(
@@ -633,22 +658,24 @@
             jax.ShapeDtypeStruct((1, N), f32),
             jax.ShapeDtypeStruct((NP, N, PK), bf16),
         ),
-        in_specs=[VM, ANY] + [VM] * 8,
+        in_specs=[VM, ANY] + [VM] * 4,
         out_specs=(VM, VM, ANY),
         scratch_shapes=[
             pltpu.VMEM((NP, PL, KO, WIDE), bf16),
-            pltpu.VMEM((2, N, PL, WIDE), bf16),
-            pltpu.VMEM((N * PL, COLS), f32),
-            pltpu.VMEM((N * PL, COLS), f32),
-            pltpu.VMEM((2, N, PK), bf16),
-            pltpu.VMEM((N, PL * COLS), bf16),
+            pltpu.VMEM((2, SHARED, PL, WIDE), bf16),
+            pltpu.VMEM((SHARED * PL, COLS), f32),
+            pltpu.VMEM((SHARED * PL, COLS), f32),
+            pltpu.VMEM((NP, N, PK), bf16),
+            pltpu.VMEM((NP, N, PL * COLS), bf16),
             pltpu.VMEM((BASES * KO, PK), bf16),
             pltpu.VMEM((KO, PL * COLS), bf16),
             pltpu.VMEM((BASES * KO, N), f32),
             pltpu.VMEM((N, KO), f32),
-            pltpu.VMEM((N, COLS), f32),
-            pltpu.VMEM((N, COLS), f32),
-            pltpu.VMEM((N, COLS), f32),
+            pltpu.VMEM((SHARED, COLS), f32),
+            pltpu.VMEM((SHARED, COLS), f32),
+            pltpu.VMEM((SHARED, COLS), f32),
+            pltpu.VMEM((SHARED, COLS), f32),
+            pltpu.VMEM((2 * PL, COLS), f32),
             pltpu.VMEM((BASES * KO, N), f32),
             pltpu.VMEM((GROUPS, 16, N), f32),
             pltpu.SemaphoreType.DMA((len(MSGS),)),
@@ -656,19 +683,19 @@
             pltpu.SemaphoreType.DMA((GROUPS,)),
             pltpu.SemaphoreType.DMA((GROUPS,)),
             pltpu.SemaphoreType.DMA((2,)),
-            pltpu.SemaphoreType.DMA((2,)),
-        ],
+        ]
+        + [pltpu.SemaphoreType.DMA((NP,))] * 5,
         compiler_params=pltpu.CompilerParams(
-            collective_id=0, has_side_effects=True, vmem_limit_bytes=40 * 2**20
+            collective_id=0, has_side_effects=True, vmem_limit_bytes=58 * 2**20
         ),
     )(
-        refs, images, focus, noise_var.reshape(NP, PL, COLS), orient_list.T, labels, rowtab, offs, coltab, lines
+        refs, images, defocus.reshape(1, N), noise_var.reshape(NP, PL, COLS), orient_list.T, class_label.reshape(1, N)
     )
     piece = SLAB_ROWS // GROUPS
     volume = pl.pallas_call(
         back_kernel,
         out_shape=jax.ShapeDtypeStruct((piece, CL * WIDE), f32),
-        in_specs=[VM, ANY] + [VM] * 6,
+        in_specs=[VM, ANY] + [VM] * 4,
         out_specs=VM,
         scratch_shapes=[
             pltpu.VMEM((3, N, PK), bf16),
@@ -690,6 +717,7 @@
             pltpu.VMEM((SIDE, piece, CL * WIDE), bf16),
             pltpu.VMEM((2, piece // 2, CL * WIDE), bf16),
             pltpu.VMEM((2, piece, CL * WIDE), bf16),
+            pltpu.VMEM((2 * PL, COLS), f32),
             pltpu.SemaphoreType.DMA((3,)),
             pltpu.SemaphoreType.DMA((CHUNKS, 16)),
             pltpu.SemaphoreType.DMA((CHUNKS, 16)),
@@ -701,7 +729,7 @@
         compiler_params=pltpu.CompilerParams(
             collective_id=1, has_side_effects=True, vmem_limit_bytes=40 * 2**20
         ),
-    )(post, weighted, coltab, lines, owner[:, :, 0], slab_row, kernel_index, interp)
+    )(post, weighted, owner[:, :, 0], slab_row, kernel_index, interp)
     return volume.reshape(piece, CL, WIDE), evidence.reshape(N)
 
 

time: 143 us -> 126 us (0.88)
  Pallas kernels: 133 us -> 120 us
  local copies, waits for them, and re-layouts: 8.92 us -> 5.11 us
    pallas_call x1, Pallas kernels: 63.4 us -> 55.3 us  [shards(): pl.pallas_call(back_kernel, out_shape=jax.ShapeDtypeStruct((piece, CL * W...]
    pallas_call x1, Pallas kernels: 70.1 us -> 64.5 us  [shards(): pl.pallas_call(score_kernel, out_shape=(jax.ShapeDtypeStruct((BASES * KO,...]
    unnamed x24 -> x12, local copies, waits for them, and re-layouts: 5.37 us -> 2.37 us
    broadcast_in_dim x2 -> x0, local copies, waits for them, and re-layouts: 1.45 us -> none  [the longest x1 0.76 us: shards(): focus = jnp.broadcast_to(defocus[:, None], (N, COLS))]
where the time goes in v3:
time: 126 us
  Pallas kernels  120 us (95%)
  local copies, waits for them, and re-layouts  5.11 us (4%)
    pallas_call x1, Pallas kernels, shards(): pl.pallas_call(score_kernel, out_shape=(jax.ShapeDtypeStruct((BASES * KO,...  64.5 us
    pallas_call x1, Pallas kernels, shards(): pl.pallas_call(back_kernel, out_shape=jax.ShapeDtypeStruct((piece, CL * W...  55.3 us

profile of v3, /device:TPU:1, one launch (start us, length us, event | category | flops | bytes accessed | tf_op | source)
XLA Modules:
  0.0 125.7 jit_solution(8549591014228255963)
XLA Ops:
  0.6 0.0 copy-start.1
  0.6 0.0 copy-start.3
  0.7 0.0 copy-start.2
  0.7 0.9 copy.15
  1.5 1.2 copy.12
  2.7 0.8 reshape.22.refs_ref
  3.5 64.5 %shard_map.113 = (bf16[288,192]{1,0:T(8,128)(2,1)}, f32[1,192]{1,0:T(1,128)}, bf16[16,192,4096]{2,1,0:T(8,128)(2,1)}) custom-call(bf16[16,32,256]{2,1,0:T(8,128)(2,1)} %reshape.22.refs_ref, bf16[192,256,256]{2,1,0:T(8,128)(2,1)} %images_hbm.1, f32[1,192]{1,0:T(1,128)} %bitcast.13, f32[16,16,128]{2,1,0:T(8,128)} %bitcast.11, s32[16,192]{1,0:T(8,128)} %bitcast.12, ...), custom_call_target="tpu_custom_call" | custom-call | tf_op jit(solution)/shard_map/pallas_call | solution.py:654
  68.0 0.0 copy-start.4
  68.0 0.0 copy-done.1
  68.0 0.0 copy-done.3
  68.0 0.0 copy-done.2
  68.0 0.0 copy-start
  68.0 0.9 copy-done
  68.9 55.3 %shard_map.114 = f32[64,1024]{1,0:T(8,128)S(1)} custom-call(bf16[288,192]{1,0:T(8,128)(2,1)S(1)} %copy-done, bf16[16,192,4096]{2,1,0:T(8,128)(2,1)} %get-tuple-element.6.weighted_hbm, s32[64,256]{1,0:T(8,128)S(1)} %bitcast.9, s32[64,256]{1,0:T(8,128)S(1)} %copy-done.2, s32[64,256]{1,0:T(8,128)S(1)} %copy-done.3, bf16[4,128,128]{2,1,0:T(8,128)(2,1)S(1)} %copy-done.1), custom_call_target="tpu_custom_call" | custom-call | tf_op jit(solution)/shard_map/pallas_call | solution.py:695
  124.3 0.8 reshape.26
  125.1 0.0 copy-done.4
  125.1 0.6 copy.17
Async XLA Ops:
  0.6 67.3 %copy-start.1 = (bf16[4,128,128]{2,1,0:T(8,128)(2,1)S(1)}, bf16[4,128,128]{2,1,0:T(8,128)(2,1)}, u32[]{:S(2)}) copy-start(bf16[4,128,128]{2,1,0:T(8,128)(2,1)} %interp_ref.1) | copy-start | bytes 393220
  0.6 67.3 %copy-start.3 = (s32[64,256]{1,0:T(8,128)S(1)}, s32[64,256]{1,0:T(8,128)}, u32[]{:S(2)}) copy-start(s32[64,256]{1,0:T(8,128)} %kernel_ref.1) | copy-start | bytes 196612
  0.7 67.3 %copy-start.2 = (s32[64,256]{1,0:T(8,128)S(1)}, s32[64,256]{1,0:T(8,128)}, u32[]{:S(2)}) copy-start(s32[64,256]{1,0:T(8,128)} %slab_ref.1) | copy-start | bytes 196612
  68.0 57.1 %copy-start.4 = (f32[1,192]{1,0:T(1,128)S(1)}, f32[1,192]{1,0:T(1,128)}, u32[]{:S(2)}) copy-start(f32[1,192]{1,0:T(1,128)} %get-tuple-element.7) | copy-start | bytes 2308
  68.0 0.9 copy-start

commit v4 on v3

--- a/solution.py
+++ b/solution.py
@@ -257,11 +257,12 @@
                 wall[step, to, j * WIDE : j * WIDE + COLS] = (fre[take, :] * fac).astype(bf16)
                 wall[step, to, j * WIDE + COLS : (j + 1) * WIDE] = (fim[take, :] * fac).astype(bf16)
                 call[step, to, j * COLS : (j + 1) * COLS] = (con * fac).astype(bf16)
+            for half in (0, 1):
+                for cp in swap(step, pl.ds(pl.multiple_of(core * SHARED + i * 32 + half * 16, 16), 16)):
+                    cp.start()
             return c
 
         lax.fori_loop(0, SHARED // 32, weigh, 0)
-        for c in swap(step, mine):
-            c.start()
 
     weigh_share(0)
 
@@ -369,13 +370,12 @@
 LAG = 2
 ROWS = PL * CL
 HALF = ROWS // 2
-QUART = ROWS // 4
 
 
 def back_kernel(
     post_ref, weighted_hbm, owner_ref, slab_ref, kernel_ref, interp_ref,
     out_ref,
-    wbuf, part, r1, r2, p2, q1, q2,
+    wbuf, part, r1, p2, q1,
     rowre, rowim, mapped, outgoing, received, placer, sender, slab, sib, chip, y1, y2, waves,
     in_sem, send_sem, recv_sem, xsend, xrecv, ysend, yrecv,
 ):
@@ -440,46 +440,28 @@
                 part[chunk, o // 2, (o % 2) * 2 + half, pl.ds(four * 16, 16), :] = piece.astype(bf16)
 
     def setup(h):
-        first, second = ("x", "z") if h == 0 else ("z", "x")
-        return (first, x, second, z) if h == 0 else (first, z, second, x)
-
-    def column(c, h, f, lo, size):
-        rows = pl.ds(h * HALF + lo, size)
+        return ("x", x, "z", z) if h == 0 else ("z", z, "x", x)
+
+    def column(c, h, f):
+        rows = pl.ds(h * HALF, HALF)
         return part.at[c, :, f, rows, :] if h == 0 else part.at[c, f, :, rows, :]
-
-    def copy(src, dst, c, idx, axis, d):
-        return pltpu.make_async_remote_copy(
-            src_ref=src, dst_ref=dst, send_sem=send_sem.at[c, idx], recv_sem=recv_sem.at[c, idx],
-            device_id=(neighbour(axis, d), group), device_id_type=MESH,
-        )
 
     def copies(c, h, stage):
         first, f, second, s = setup(h)
-        far_f, far_s = (f + 2) % 4, (s + 2) % 4
         out = []
-        for n_, d in enumerate((3, 1)):
-            idx = (h * 4 + stage) * 2 + n_
+        for k in (2, 1, 3):
+            idx = (h * 2 + stage) * 3 + k - 1
             if stage == 0:
-                out.append(copy(column(c, h, far_f, n_ * QUART, QUART), r1.at[c, h, n_], c, idx, first, d))
-            elif stage == 1:
-                out.append(copy(column(c, h, (f + d) % 4, 0, HALF), r2.at[c, h, n_], c, idx, first, d))
-            elif stage == 2:
-                src = p2.at[c, h, far_s, pl.ds(n_ * QUART, QUART), :]
-                out.append(copy(src, q1.at[c, h, n_], c, idx, second, d))
+                src, dst, axis = column(c, h, (f + k) % SIDE), r1.at[c, h, k - 1], first
             else:
-                out.append(copy(p2.at[c, h, (s + d) % 4], q2.at[c, h, n_], c, idx, second, d))
+                src, dst, axis = p2.at[c, h, (s + k) % SIDE], q1.at[c, h, k - 1], second
+            out.append(
+                pltpu.make_async_remote_copy(
+                    src_ref=src, dst_ref=dst, send_sem=send_sem.at[c, idx], recv_sem=recv_sem.at[c, idx],
+                    device_id=(neighbour(axis, k), group), device_id_type=MESH,
+                )
+            )
         return out
-
-    def column_get(c, h, f, i, lo, size):
-        rows = pl.ds(h * HALF + lo, size)
-        return part[c, i, f, rows, :] if h == 0 else part[c, f, i, rows, :]
-
-    def column_set(c, h, f, i, lo, size, value):
-        rows = pl.ds(h * HALF + lo, size)
-        if h == 0:
-            part[c, i, f, rows, :] = value
-        else:
-            part[c, f, i, rows, :] = value
 
     def advance(c, stage):
         for h in (0, 1):
@@ -488,30 +470,21 @@
                 for cp_ in copies(c, h, stage - 1):
                     cp_.wait_recv()
             if stage == 1:
-                for n_, d in enumerate((3, 1)):
-                    for i in range(SIDE):
-                        to = (f + d) % 4
-                        mine = column_get(c, h, to, i, n_ * QUART, QUART).astype(f32)
-                        new = mine + r1[c, h, n_, i].astype(f32)
-                        column_set(c, h, to, i, n_ * QUART, QUART, new.astype(bf16))
+                for i in range(SIDE):
+                    rows = pl.ds(h * HALF, HALF)
+                    new = (part[c, i, f, rows, :] if h == 0 else part[c, f, i, rows, :]).astype(f32)
+                    for k in range(3):
+                        new = new + r1[c, h, k, i].astype(f32)
+                    p2[c, h, i] = new.astype(bf16)
             elif stage == 2:
-                for i in range(SIDE):
-                    new = column_get(c, h, f, i, 0, HALF).astype(f32)
-                    new = new + r2[c, h, 0, i].astype(f32) + r2[c, h, 1, i].astype(f32)
-                    p2[c, h, i] = new.astype(bf16)
-            elif stage == 3:
-                for n_, d in enumerate((3, 1)):
-                    rows = pl.ds(n_ * QUART, QUART)
-                    to = (s + d) % 4
-                    new = p2[c, h, to, rows, :].astype(f32) + q1[c, h, n_].astype(f32)
-                    p2[c, h, to, rows, :] = new.astype(bf16)
-            elif stage == 4:
-                new = p2[c, h, s].astype(f32) + q2[c, h, 0].astype(f32) + q2[c, h, 1].astype(f32)
+                new = p2[c, h, s].astype(f32)
+                for k in range(3):
+                    new = new + q1[c, h, k].astype(f32)
                 new = new.astype(bf16).astype(f32)
                 rows = pl.ds(pl.multiple_of(c * ROWS, ROWS) + h * HALF, HALF)
                 rowre[rows, :] = new[:, :COLS]
                 rowim[rows, :] = new[:, COLS:]
-            if stage < 4:
+            if stage < 2:
                 for cp_ in copies(c, h, stage):
                     cp_.start()
 
@@ -562,12 +535,12 @@
             lax.fori_loop(0, 2, body, 0)
 
         pl.when(t == CHUNKS)(prepare)
-        for stage in range(5):
+        for stage in range(3):
             c = t - LAG * stage
             pl.when((c >= 0) & (c < CHUNKS))(functools.partial(advance, c, stage))
         return carry
 
-    lax.fori_loop(0, CHUNKS + 4 * LAG, tick, 0)
+    lax.fori_loop(0, CHUNKS + 2 * LAG, tick, 0)
 
     for k in range(CL):
         for n_, ref in enumerate((rowre, rowim)):
@@ -633,7 +606,7 @@
 
     for c in range(CHUNKS):
         for h in (0, 1):
-            for stage in range(4):
+            for stage in range(2):
                 for cp_ in copies(c, h, stage):
                     cp_.wait_send()
     for k in range(1, NP):
@@ -700,11 +673,9 @@
         scratch_shapes=[
             pltpu.VMEM((3, N, PK), bf16),
             pltpu.VMEM((CHUNKS, SIDE, SIDE, ROWS, WIDE), bf16),
-            pltpu.VMEM((CHUNKS, 2, 2, SIDE, QUART, WIDE), bf16),
-            pltpu.VMEM((CHUNKS, 2, 2, SIDE, HALF, WIDE), bf16),
+            pltpu.VMEM((CHUNKS, 2, 3, SIDE, HALF, WIDE), bf16),
             pltpu.VMEM((CHUNKS, 2, SIDE, HALF, WIDE), bf16),
-            pltpu.VMEM((CHUNKS, 2, 2, QUART, WIDE), bf16),
-            pltpu.VMEM((CHUNKS, 2, 2, HALF, WIDE), bf16),
+            pltpu.VMEM((CHUNKS, 2, 3, HALF, WIDE), bf16),
             pltpu.VMEM((CHUNKS * ROWS, COLS), f32),
             pltpu.VMEM((CHUNKS * ROWS, COLS), f32),
             pltpu.VMEM((4 * COLS, CL * WIDE), bf16),
@@ -719,8 +690,8 @@
             pltpu.VMEM((2, piece, CL * WIDE), bf16),
             pltpu.VMEM((2 * PL, COLS), f32),
             pltpu.SemaphoreType.DMA((3,)),
-            pltpu.SemaphoreType.DMA((CHUNKS, 16)),
-            pltpu.SemaphoreType.DMA((CHUNKS, 16)),
+            pltpu.SemaphoreType.DMA((CHUNKS, 12)),
+            pltpu.SemaphoreType.DMA((CHUNKS, 12)),
             pltpu.SemaphoreType.DMA((NP,)),
             pltpu.SemaphoreType.DMA((NP,)),
             pltpu.SemaphoreType.DMA((5,)),

time: 126 us -> 128 us (1.016)
  Pallas kernels: 120 us -> 122 us
    pallas_call x1, Pallas kernels: 55.3 us -> 57.6 us  [shards(): pl.pallas_call(back_kernel, out_shape=jax.ShapeDtypeStruct((piece, CL * W...]
where the time goes in v4:
time: 128 us
  Pallas kernels  122 us (95%)
  local copies, waits for them, and re-layouts  5.11 us (4%)
    pallas_call x1, Pallas kernels, shards(): pl.pallas_call(score_kernel, out_shape=(jax.ShapeDtypeStruct((BASES * KO,...  64.7 us
    pallas_call x1, Pallas kernels, shards(): pl.pallas_call(back_kernel, out_shape=jax.ShapeDtypeStruct((piece, CL * W...  57.6 us

profile of v4, /device:TPU:1, one launch (start us, length us, event | category | flops | bytes accessed | tf_op | source)
XLA Modules:
  0.0 128.2 jit_solution(754101839182312690)
XLA Ops:
  0.6 0.0 copy-start.1
  0.6 0.0 copy-start.3
  0.7 0.0 copy-start.2
  0.7 0.9 copy.15
  1.5 1.2 copy.12
  2.7 0.8 reshape.22.refs_ref
  3.5 64.7 %shard_map.113 = (bf16[288,192]{1,0:T(8,128)(2,1)}, f32[1,192]{1,0:T(1,128)}, bf16[16,192,4096]{2,1,0:T(8,128)(2,1)}) custom-call(bf16[16,32,256]{2,1,0:T(8,128)(2,1)} %reshape.22.refs_ref, bf16[192,256,256]{2,1,0:T(8,128)(2,1)} %images_hbm.1, f32[1,192]{1,0:T(1,128)} %bitcast.13, f32[16,16,128]{2,1,0:T(8,128)} %bitcast.11, s32[16,192]{1,0:T(8,128)} %bitcast.12, ...), custom_call_target="tpu_custom_call" | custom-call | tf_op jit(solution)/shard_map/pallas_call | solution.py:627
  68.2 0.0 copy-start.4
  68.2 0.0 copy-done.1
  68.2 0.0 copy-done.3
  68.2 0.0 copy-done.2
  68.2 0.0 copy-start
  68.2 0.9 copy-done
  69.1 57.6 %shard_map.114 = f32[64,1024]{1,0:T(8,128)S(1)} custom-call(bf16[288,192]{1,0:T(8,128)(2,1)S(1)} %copy-done, bf16[16,192,4096]{2,1,0:T(8,128)(2,1)} %get-tuple-element.6.weighted_hbm, s32[64,256]{1,0:T(8,128)S(1)} %bitcast.9, s32[64,256]{1,0:T(8,128)S(1)} %copy-done.2, s32[64,256]{1,0:T(8,128)S(1)} %copy-done.3, bf16[4,128,128]{2,1,0:T(8,128)(2,1)S(1)} %copy-done.1), custom_call_target="tpu_custom_call" | custom-call | tf_op jit(solution)/shard_map/pallas_call | solution.py:668
  126.8 0.8 reshape.26
  127.6 0.0 copy-done.4
  127.6 0.6 copy.17
Async XLA Ops:
  0.6 67.6 %copy-start.1 = (bf16[4,128,128]{2,1,0:T(8,128)(2,1)S(1)}, bf16[4,128,128]{2,1,0:T(8,128)(2,1)}, u32[]{:S(2)}) copy-start(bf16[4,128,128]{2,1,0:T(8,128)(2,1)} %interp_ref.1) | copy-start | bytes 393220
  0.6 67.6 %copy-start.3 = (s32[64,256]{1,0:T(8,128)S(1)}, s32[64,256]{1,0:T(8,128)}, u32[]{:S(2)}) copy-start(s32[64,256]{1,0:T(8,128)} %kernel_ref.1) | copy-start | bytes 196612
  0.7 67.6 %copy-start.2 = (s32[64,256]{1,0:T(8,128)S(1)}, s32[64,256]{1,0:T(8,128)}, u32[]{:S(2)}) copy-start(s32[64,256]{1,0:T(8,128)} %slab_ref.1) | copy-start | bytes 196612
  68.2 59.4 %copy-start.4 = (f32[1,192]{1,0:T(1,128)S(1)}, f32[1,192]{1,0:T(1,128)}, u32[]{:S(2)}) copy-start(f32[1,192]{1,0:T(1,128)} %get-tuple-element.7) | copy-start | bytes 2308
  68.2 0.9 copy-start

commit v5 on v3

--- a/solution.py
+++ b/solution.py
@@ -23,6 +23,7 @@
 SIDE = 4
 GROUPS = 8
 BASES = 9
+AHEAD = 2
 SHARED = N // 2
 CAP = 16
 
@@ -263,10 +264,11 @@
         for c in swap(step, mine):
             c.start()
 
-    weigh_share(0)
+    for i in range(AHEAD):
+        weigh_share(i)
 
     def one_share(step, carry):
-        pl.when(step + 1 < NP)(lambda: weigh_share(step + 1))
+        pl.when(step + AHEAD < NP)(lambda: weigh_share(step + AHEAD))
         for i in range(1, NP):
             if STEPS[i]:
                 pl.when(step == i)(functools.partial(traffic, STEPS[i]))

time: 126 us -> 125 us (level)
  no operation moved by 1% of the time
where the time goes in v5:
time: 125 us; the launch traced here: 124 us
  Pallas kernels  119 us (95%)
  local copies, waits for them, and re-layouts  5.11 us (4%)
    pallas_call x1, Pallas kernels, shards(): pl.pallas_call(score_kernel, out_shape=(jax.ShapeDtypeStruct((BASES * KO,...  63.8 us
    pallas_call x1, Pallas kernels, shards(): pl.pallas_call(back_kernel, out_shape=jax.ShapeDtypeStruct((piece, CL * W...  54.8 us

profile of v5, /device:TPU:1, one launch (start us, length us, event | category | flops | bytes accessed | tf_op | source)
XLA Modules:
  0.0 124.4 jit_solution(1250394181418461760)
XLA Ops:
  0.6 0.0 copy-start.1
  0.6 0.0 copy-start.3
  0.7 0.0 copy-start.2
  0.7 0.9 copy.15
  1.5 1.2 copy.12
  2.7 0.8 reshape.22.refs_ref
  3.5 63.8 %shard_map.113 = (bf16[288,192]{1,0:T(8,128)(2,1)}, f32[1,192]{1,0:T(1,128)}, bf16[16,192,4096]{2,1,0:T(8,128)(2,1)}) custom-call(bf16[16,32,256]{2,1,0:T(8,128)(2,1)} %reshape.22.refs_ref, bf16[192,256,256]{2,1,0:T(8,128)(2,1)} %images_hbm.1, f32[1,192]{1,0:T(1,128)} %bitcast.13, f32[16,16,128]{2,1,0:T(8,128)} %bitcast.11, s32[16,192]{1,0:T(8,128)} %bitcast.12, ...), custom_call_target="tpu_custom_call" | custom-call | tf_op jit(solution)/shard_map/pallas_call | solution.py:656
  67.2 0.0 copy-start.4
  67.2 0.0 copy-done.1
  67.3 0.0 copy-done.3
  67.3 0.0 copy-done.2
  67.3 0.0 copy-start
  67.3 0.9 copy-done
  68.2 54.8 %shard_map.114 = f32[64,1024]{1,0:T(8,128)S(1)} custom-call(bf16[288,192]{1,0:T(8,128)(2,1)S(1)} %copy-done, bf16[16,192,4096]{2,1,0:T(8,128)(2,1)} %get-tuple-element.6.weighted_hbm, s32[64,256]{1,0:T(8,128)S(1)} %bitcast.9, s32[64,256]{1,0:T(8,128)S(1)} %copy-done.2, s32[64,256]{1,0:T(8,128)S(1)} %copy-done.3, bf16[4,128,128]{2,1,0:T(8,128)(2,1)S(1)} %copy-done.1), custom_call_target="tpu_custom_call" | custom-call | tf_op jit(solution)/shard_map/pallas_call | solution.py:697
  123.0 0.8 reshape.26
  123.8 0.0 copy-done.4
  123.8 0.6 copy.17
Async XLA Ops:
  0.6 66.6 %copy-start.1 = (bf16[4,128,128]{2,1,0:T(8,128)(2,1)S(1)}, bf16[4,128,128]{2,1,0:T(8,128)(2,1)}, u32[]{:S(2)}) copy-start(bf16[4,128,128]{2,1,0:T(8,128)(2,1)} %interp_ref.1) | copy-start | bytes 393220
  0.6 66.6 %copy-start.3 = (s32[64,256]{1,0:T(8,128)S(1)}, s32[64,256]{1,0:T(8,128)}, u32[]{:S(2)}) copy-start(s32[64,256]{1,0:T(8,128)} %kernel_ref.1) | copy-start | bytes 196612
  0.7 66.6 %copy-start.2 = (s32[64,256]{1,0:T(8,128)S(1)}, s32[64,256]{1,0:T(8,128)}, u32[]{:S(2)}) copy-start(s32[64,256]{1,0:T(8,128)} %slab_ref.1) | copy-start | bytes 196612
  67.2 56.6 %copy-start.4 = (f32[1,192]{1,0:T(1,128)S(1)}, f32[1,192]{1,0:T(1,128)}, u32[]{:S(2)}) copy-start(f32[1,192]{1,0:T(1,128)} %get-tuple-element.7) | copy-start | bytes 2308
  67.3 0.9 copy-start

commit v6 on v5

--- a/solution.py
+++ b/solution.py
@@ -555,18 +555,17 @@
             sender[:, w * COLS : (w + 1) * COLS] = jnp.where(hit & (kern == w), 1.0, 0.0).astype(bf16)
 
     def tick(t, carry):
+        pl.when(t < CHUNKS)(lambda: compute(t * 2))
+        for stage in range(1, 5):
+            c = t - LAG * stage
+            pl.when((c >= 0) & (c < CHUNKS))(functools.partial(advance, c, stage))
+        pl.when(t == CHUNKS)(prepare)
+
         @pl.when(t < CHUNKS)
         def _():
-            def body(q, c):
-                compute(t * 2 + q)
-                return c
-
-            lax.fori_loop(0, 2, body, 0)
-
-        pl.when(t == CHUNKS)(prepare)
-        for stage in range(5):
-            c = t - LAG * stage
-            pl.when((c >= 0) & (c < CHUNKS))(functools.partial(advance, c, stage))
+            compute(t * 2 + 1)
+            advance(t, 0)
+
         return carry
 
     lax.fori_loop(0, CHUNKS + 4 * LAG, tick, 0)

time: 125 us -> 127 us (1.016)
  Pallas kernels: 119 us -> 121 us
    pallas_call x1, Pallas kernels: 54.8 us -> 57.6 us  [shards(): pl.pallas_call(back_kernel, out_shape=jax.ShapeDtypeStruct((piece, CL * W...]
where the time goes in v6:
time: 127 us
  Pallas kernels  121 us (95%)
  local copies, waits for them, and re-layouts  5.11 us (4%)
    pallas_call x1, Pallas kernels, shards(): pl.pallas_call(score_kernel, out_shape=(jax.ShapeDtypeStruct((BASES * KO,...  63.8 us
    pallas_call x1, Pallas kernels, shards(): pl.pallas_call(back_kernel, out_shape=jax.ShapeDtypeStruct((piece, CL * W...  57.6 us

profile of v6, /device:TPU:1, one launch (start us, length us, event | category | flops | bytes accessed | tf_op | source)
XLA Modules:
  0.0 127.2 jit_solution(1926151176434755246)
XLA Ops:
  0.6 0.0 copy-start.1
  0.6 0.0 copy-start.3
  0.7 0.0 copy-start.2
  0.7 0.9 copy.15
  1.5 1.2 copy.12
  2.7 0.8 reshape.22.refs_ref
  3.5 63.8 %shard_map.113 = (bf16[288,192]{1,0:T(8,128)(2,1)}, f32[1,192]{1,0:T(1,128)}, bf16[16,192,4096]{2,1,0:T(8,128)(2,1)}) custom-call(bf16[16,32,256]{2,1,0:T(8,128)(2,1)} %reshape.22.refs_ref, bf16[192,256,256]{2,1,0:T(8,128)(2,1)} %images_hbm.1, f32[1,192]{1,0:T(1,128)} %bitcast.13, f32[16,16,128]{2,1,0:T(8,128)} %bitcast.11, s32[16,192]{1,0:T(8,128)} %bitcast.12, ...), custom_call_target="tpu_custom_call" | custom-call | tf_op jit(solution)/shard_map/pallas_call | solution.py:655
  67.2 0.0 copy-start.4
  67.2 0.0 copy-done.1
  67.3 0.0 copy-done.3
  67.3 0.0 copy-done.2
  67.3 0.0 copy-start
  67.3 0.9 copy-done
  68.2 57.6 %shard_map.114 = f32[64,1024]{1,0:T(8,128)S(1)} custom-call(bf16[288,192]{1,0:T(8,128)(2,1)S(1)} %copy-done, bf16[16,192,4096]{2,1,0:T(8,128)(2,1)} %get-tuple-element.6.weighted_hbm, s32[64,256]{1,0:T(8,128)S(1)} %bitcast.9, s32[64,256]{1,0:T(8,128)S(1)} %copy-done.2, s32[64,256]{1,0:T(8,128)S(1)} %copy-done.3, bf16[4,128,128]{2,1,0:T(8,128)(2,1)S(1)} %copy-done.1), custom_call_target="tpu_custom_call" | custom-call | tf_op jit(solution)/shard_map/pallas_call | solution.py:696
  125.8 0.8 reshape.26
  126.6 0.0 copy-done.4
  126.6 0.6 copy.17
Async XLA Ops:
  0.6 66.6 %copy-start.1 = (bf16[4,128,128]{2,1,0:T(8,128)(2,1)S(1)}, bf16[4,128,128]{2,1,0:T(8,128)(2,1)}, u32[]{:S(2)}) copy-start(bf16[4,128,128]{2,1,0:T(8,128)(2,1)} %interp_ref.1) | copy-start | bytes 393220
  0.6 66.6 %copy-start.3 = (s32[64,256]{1,0:T(8,128)S(1)}, s32[64,256]{1,0:T(8,128)}, u32[]{:S(2)}) copy-start(s32[64,256]{1,0:T(8,128)} %kernel_ref.1) | copy-start | bytes 196612
  0.7 66.6 %copy-start.2 = (s32[64,256]{1,0:T(8,128)S(1)}, s32[64,256]{1,0:T(8,128)}, u32[]{:S(2)}) copy-start(s32[64,256]{1,0:T(8,128)} %slab_ref.1) | copy-start | bytes 196612
  67.2 59.4 %copy-start.4 = (f32[1,192]{1,0:T(1,128)S(1)}, f32[1,192]{1,0:T(1,128)}, u32[]{:S(2)}) copy-start(f32[1,192]{1,0:T(1,128)} %get-tuple-element.7) | copy-start | bytes 2308
  67.3 0.9 copy-start
